TPU v7x, 32 devices: a whole 2x2x4 slice. The times are simulated.
32 devices in a mesh: start: 2 (over core), pencil: 16 (over z, y, x).
Axes of the slice: x: 2, y: 2, z: 4, core: 2. Of those that a mesh axis runs over, the one named last changes fastest.
Arguments:
- template: bfloat16 [64, 64, 512], P('pencil', 'start'), parts along dimension 1, may hold values from -3.5 to 3.5
- reference_image: bfloat16 [64, 64, 512], P('pencil', 'start'), parts along dimension 1, may hold values from -3.5 to 3.5
- velocity: float32 [6, 64, 32, 512], P('start', 'pencil'), parts along dimension 0, may hold values from -4 to 4
- dep_owner: int32 [4, 4096], P('start', 'pencil'), parts along dimension 0, may hold values from 0 to 15, as said below
- dep_offset: int32 [4, 4096], P('start', 'pencil'), parts along dimension 0, may hold values from 0 to 255
- dep_weight: int32 [4, 4096], P('start', 'pencil'), parts along dimension 0, may hold values from 0 to 15
Outputs:
- warped: bfloat16 [64, 64, 512], P('pencil', 'start'), parts along dimension 1
- gradient: float32 [6, 64, 32, 512], P('start', 'pencil'), parts along dimension 0
There are 2 independent parts, one for each index of `start`. A program takes and returns all parts, laid end to end along the dimension named above; each array names one. Nothing has to cross between parts.
Inputs may be any that keep to these rules, and one draw needn't show every extreme that they name: Device d holds blocks d * 256 to (d + 1) * 256 - 1. For a block of device d, dep_owner is (d + m) mod 16 with m one of -2, -1, 0, 1, so that its stencil rows lie on devices d - 2 to d + 2 (modulo 16).
All inputs are finite; a program needn't handle non-finite values.
Results may differ from a plain program's by a relative error of at most 0.012.
Values may be sent and summed in bfloat16 or wider, within the bound.
A program may use at most 192 MiB of HBM per device.

v0:
```python
import math

import jax
import jax.numpy as jnp
from jax import lax
from jax.sharding import PartitionSpec as P

ZB = 2
SEG = 128
Q = 16


h1_weight = 64.0
force_gain = 32.0


def shifted(x, axis, by):
    length = lax.axis_size(axis)
    return lax.ppermute(x, axis, [(i, (i + by) % length) for i in range(length)])


def dft_tables(length):
    series = jnp.arange(length, dtype=jnp.int32)
    product = series[:, None] * series[None, :] % length
    angles = product.astype(jnp.float32) * (2.0 * math.pi / length)
    return (jnp.cos(angles).astype(jnp.bfloat16), jnp.sin(angles).astype(jnp.bfloat16))


def signed_waves(series, length):
    signed = jnp.where(series < length // 2, series, series - length)
    signed = jnp.where(series == length // 2, 0, signed)
    return signed.astype(jnp.float32) * (2.0 * math.pi / length)


def wave_numbers(length):
    return signed_waves(jnp.arange(length, dtype=jnp.int32), length)


def cubic_table(levels):
    fraction = (jnp.arange(levels, dtype=jnp.float32) + 0.5) / levels
    node_left = -fraction * (fraction - 1.0) * (fraction - 2.0) / 6.0
    node_zero = (fraction + 1.0) * (fraction - 1.0) * (fraction - 2.0) / 2.0
    node_one = -(fraction + 1.0) * fraction * (fraction - 2.0) / 2.0
    node_two = (fraction + 1.0) * fraction * (fraction - 1.0) / 6.0
    return jnp.stack([node_left, node_zero, node_one, node_two], axis=1)


def pick_weights(weight_level, weight_table):
    onehot = (
        weight_level[:, None] == jnp.arange(weight_table.shape[0], dtype=jnp.int32)[None, :]
    ).astype(jnp.float32)
    return jnp.dot(onehot, weight_table, precision=lax.Precision.HIGHEST)


def local(template, reference_image, velocity, dep_owner, dep_offset, dep_weight):
    peer_count = lax.axis_size("pencil")
    row_count, plane_count, y_count = template.shape
    full_rows = row_count * peer_count
    z_groups = plane_count // ZB
    y_groups = y_count // SEG
    per_row = z_groups * y_groups
    block_count = row_count * per_row
    cell_count = plane_count * y_count
    weight_table = cubic_table(Q)
    my_index = lax.axis_index("pencil")
    shaped = template.reshape(row_count, z_groups, ZB, y_groups, SEG)
    blocks = shaped.transpose(0, 1, 3, 2, 4).reshape(block_count, ZB * SEG)
    for section_index in range(2):
        pieces = []
        for distance in (2, 1, 0, -1, -2):
            if distance == 0:
                pieces.append(blocks)
            else:
                pieces.append(shifted(blocks, "pencil", distance))
        window = jnp.concatenate(pieces, axis=0)
        relative = (dep_owner[section_index] - my_index + peer_count) % peer_count
        move = jnp.where(relative >= peer_count - 2, relative - peer_count, relative)
        offset = dep_offset[section_index]
        start_row = offset // per_row
        place = offset % per_row
        tap_row = (
            (move[:, None] + 2) * row_count
            + start_row[:, None]
            + jnp.arange(4, dtype=jnp.int32)[None, :]
        )
        taps = window[tap_row * per_row + place[:, None]].astype(jnp.float32)
        weights = pick_weights(dep_weight[section_index], weight_table)
        blocks = jnp.sum(weights[:, :, None] * taps, axis=1).astype(jnp.bfloat16)
    shaped = blocks.reshape(row_count, z_groups, y_groups, ZB, SEG)
    warped = shaped.transpose(0, 1, 3, 2, 4).reshape(row_count, plane_count, y_count)
    warped_f = warped.astype(jnp.float32)
    residual = reference_image.astype(jnp.float32) - warped_f
    cos_y, sin_y = dft_tables(y_count)
    cos_x, sin_x = dft_tables(full_rows)
    kvec_y = wave_numbers(y_count)
    kvec_x = wave_numbers(full_rows)
    forward_y = jnp.concatenate([cos_y, -sin_y], axis=1)
    inverse_y = jnp.concatenate([cos_y, -sin_y], axis=0)
    forward_x = jnp.concatenate([cos_x, -sin_x], axis=0)
    inverse_x = jnp.concatenate([cos_x, -sin_x], axis=1)
    spec_y = jnp.dot(warped.reshape(-1, y_count), forward_y, preferred_element_type=jnp.float32)
    spec_y = spec_y.astype(jnp.bfloat16).astype(jnp.float32)
    coef_y = jnp.concatenate(
        [-kvec_y * spec_y[:, y_count:], kvec_y * spec_y[:, :y_count]], axis=1
    ).astype(jnp.bfloat16)
    slope_y = (jnp.dot(coef_y, inverse_y, preferred_element_type=jnp.float32) / y_count).reshape(
        row_count, plane_count, y_count
    )
    flat_warp = warped.reshape(1, row_count, cell_count)
    spec_x = jnp.einsum(
        "kx,ixm->ikm",
        forward_x,
        lax.all_to_all(flat_warp, "pencil", split_axis=2, concat_axis=1, tiled=True),
        preferred_element_type=jnp.float32,
    )
    coef_x = jnp.concatenate(
        [
            -kvec_x[None, :, None] * spec_x[:, full_rows:],
            kvec_x[None, :, None] * spec_x[:, :full_rows],
        ],
        axis=1,
    ).astype(jnp.bfloat16)
    slope = (
        jnp.einsum("xk,ikm->ixm", inverse_x, coef_x, preferred_element_type=jnp.float32) / full_rows
    ).astype(jnp.bfloat16)
    slope_x = lax.all_to_all(slope, "pencil", split_axis=1, concat_axis=2, tiled=True)
    slope_x = slope_x.reshape(row_count, plane_count, y_count)
    slope_z = (jnp.roll(warped_f, -1, axis=1) - jnp.roll(warped_f, 1, axis=1)) * 0.5
    force = (jnp.stack([slope_x.astype(jnp.float32), slope_y, slope_z]) * residual[None]).astype(
        jnp.bfloat16
    )
    force_lines = force.reshape(-1, y_count)
    spec_real = jnp.dot(force_lines, cos_y, preferred_element_type=jnp.float32).astype(jnp.bfloat16)
    spec_imag = jnp.dot(force_lines, -sin_y, preferred_element_type=jnp.float32).astype(
        jnp.bfloat16
    )
    spec_f = jnp.stack(
        [spec_real.reshape(3, row_count, cell_count), spec_imag.reshape(3, row_count, cell_count)],
        axis=1,
    )
    planes = lax.all_to_all(spec_f, "pencil", split_axis=3, concat_axis=2, tiled=True)
    local_cols = planes.shape[3]
    column_ids = my_index * local_cols + jnp.arange(local_cols, dtype=jnp.int32)
    kvec_local = signed_waves(column_ids % y_count, y_count)
    spectral_gain = force_gain / (
        full_rows
        * y_count
        * (
            1.0
            + h1_weight
            * (kvec_x[:, None] * kvec_x[:, None] + kvec_local[None, :] * kvec_local[None, :])
        )
    )
    cos_part = jnp.einsum("kx,chxm->chkm", cos_x, planes, preferred_element_type=jnp.float32)
    sin_part = jnp.einsum("kx,chxm->chkm", sin_x, planes, preferred_element_type=jnp.float32)
    real_f = cos_part[:, 0] + sin_part[:, 1]
    imag_f = cos_part[:, 1] - sin_part[:, 0]
    scale_grid = spectral_gain[None]
    scaled = jnp.stack([real_f * scale_grid, imag_f * scale_grid], axis=1).astype(jnp.bfloat16)
    cos_back = jnp.einsum("xk,chkm->chxm", cos_x, scaled, preferred_element_type=jnp.float32)
    sin_back = jnp.einsum("xk,chkm->chxm", sin_x, scaled, preferred_element_type=jnp.float32)
    real_b = cos_back[:, 0] - sin_back[:, 1]
    imag_b = cos_back[:, 1] + sin_back[:, 0]
    mixed = jnp.stack([real_b, imag_b], axis=1).astype(jnp.bfloat16)
    smoothed = lax.all_to_all(mixed, "pencil", split_axis=2, concat_axis=3, tiled=True)
    spatial = jnp.dot(
        smoothed[:, 0].reshape(-1, y_count), cos_y, preferred_element_type=jnp.float32
    )
    spatial = spatial - jnp.dot(
        smoothed[:, 1].reshape(-1, y_count), sin_y, preferred_element_type=jnp.float32
    )
    gradient = velocity + spatial.reshape(3, row_count, plane_count, y_count)
    return (warped, gradient)


def solution(mesh):
    in_specs = (
        P("pencil", "start", None),
        P("pencil", "start", None),
        P("start", "pencil", None, None),
        P("start", "pencil"),
        P("start", "pencil"),
        P("start", "pencil"),
    )
    out_specs = (P("pencil", "start", None), P("start", "pencil", None, None))
    return jax.shard_map(local, mesh=mesh, in_specs=in_specs, out_specs=out_specs, check_vma=False)
```

profile of v0, /device:TPU:0, one launch (start us, length us, event | category | flops | bytes accessed | tf_op | source)
XLA Modules:
  0.0 596.8 jit_solution(11875163990959664800)
XLA Ops:
  0.6 0.9 reshape.587
  1.7 3.0 collective-permute-start
  4.7 1.5 collective-permute-start.1
  6.2 4.1 collective-permute-start.2
  10.4 0.4 collective-permute-start.3
  10.8 3.9 cosine_convert_fusion
  14.7 4.0 fusion.22
  18.7 0.8 fusion.127
  19.5 0.8 subtract_add_fusion
  20.9 0.3 fusion.41
  21.4 0.7 cosine_convert_fusion.3
  22.1 0.8 fusion.60
  23.0 3.9 gather_fusion
  27.2 0.7 multiply_reduce_fusion.1
  28.0 1.7 collective-permute-start.4
  29.7 5.6 collective-permute-start.6
  35.3 0.9 collective-permute-start.7
  36.2 0.4 collective-permute-done.4
  36.6 2.0 collective-permute-done.5
  38.7 2.6 collective-permute-done.7
  41.3 3.9 gather_fusion.1
  45.5 0.7 multiply_reduce_fusion
  46.5 13.0 %copy.79 = bf16[1,4,16384]{1,0,2:T(2,128)(2,1)} copy(bf16[1,4,16384]{2,1,0:T(4,128)(2,1)S(1)} %reshape_reshape.6) | data formatting | bytes 262144 | tf_op jit(solution)/shard_map/reshape;reshape | solution.py:109
  59.4 0.5 broadcast.912
  60.0 90.8 %reduce = bf16[16384,4]{1,0:T(8,128)(2,1)} reduce(bf16[16384,1,4]{2,1,0:T(2,128)(2,1)} %bitcast.110, bf16[]{:T(256)} %broadcast.912), dimensions={1}, to_apply=%bitcast.88.reduce_sub_computation | reduce | bytes 262146
  150.7 9.3 %reshape.616 = bf16[16,2,2048]{2,1,0:T(2,128)(2,1)} reshape(bf16[16384,4]{1,0:T(8,128)(2,1)} %reduce) | data formatting | bytes 262144
  160.1 5.2 all-to-all-start
  165.3 0.3 fusion
  165.7 0.3 convolution_multiply_fusion.1
  166.1 7.0 %all-to-all-done = bf16[16,2,2048]{2,1,0:T(2,128)(2,1)S(1)} async-done(((bf16[16,2,2048]{2,1,0:T(2,128)(2,1)}), bf16[16,2,2048]{2,1,0:T(2,128)(2,1)S(1)}, u32[]{:S(2)}, u32[]{:S(2)}) %all-to-all-start) | async-done | bytes 131104 | tf_op jit(solution)/shard_map/all_to_all | solution.py:113
  173.1 12.3 %reshape.617 = bf16[16384,1,4]{2,1,0:T(2,128)(2,1)} reshape(bf16[16,2,2048]{2,1,0:T(2,128)(2,1)S(1)} %all-to-all-done) | data formatting | bytes 262144
  185.4 15.4 %copy.80 = bf16[1,4,16384]{2,1,0:T(4,128)(2,1)S(1)} copy(bf16[1,4,16384]{1,0,2:T(2,128)(2,1)} %bitcast.111) | data formatting | bytes 262144 | tf_op jit(solution)/shard_map/all_to_all | solution.py:113
  201.8 1.4 reduce.1
  203.1 0.7 reshape.618
  203.9 3.5 all-to-all-start.1
  207.5 7.6 %all-to-all-done.1 = bf16[16,2,2048]{2,1,0:T(2,128)(2,1)S(1)} async-done(((bf16[16,2,2048]{2,1,0:T(2,128)(2,1)}), bf16[16,2,2048]{2,1,0:T(2,128)(2,1)S(1)}, u32[]{:S(2)}, u32[]{:S(2)}) %all-to-all-start.1) | async-done | bytes 131104 | tf_op jit(solution)/shard_map/all_to_all | solution.py:126
  215.6 4.8 convolution_convert_fusion.1
  220.5 4.9 convolution_convert_fusion
  225.3 0.3 stack_reshape.10
  225.6 39.3 %copy.85 = bf16[3,1,4,16384]{2,1,0,3:T(2,128)(2,1)} copy(bf16[3,1,4,16384]{3,2,0,1:T(4,128)(2,1)S(1)} %stack_reshape.10) | data formatting | bytes 786432 | tf_op jit(solution)/shard_map/stack;reshape | solution.py:137
  265.0 0.3 stack_reshape.11
  265.3 39.6 %copy.86 = bf16[3,1,4,16384]{2,1,0,3:T(2,128)(2,1)} copy(bf16[3,1,4,16384]{3,2,0,1:T(4,128)(2,1)S(1)} %stack_reshape.11) | data formatting | bytes 786432 | tf_op jit(solution)/shard_map/stack;reshape | solution.py:137
  304.9 70.4 %fusion.128 = bf16[16384,3,2,4]{3,2,1,0:T(2,128)(2,1)} fusion(bf16[3,1,4,16384]{2,1,0,3:T(2,128)(2,1)} %copy.86, bf16[3,1,4,16384]{2,1,0,3:T(2,128)(2,1)} %copy.85), kind=kLoop, calls=%fused_computation.233 | loop fusion | flops 1572864 | bytes 1572864
  375.3 49.6 %reshape.620 = bf16[16,2,12288]{2,1,0:T(2,128)(2,1)} reshape(bf16[16384,3,2,4]{3,2,1,0:T(2,128)(2,1)} %fusion.128) | data formatting | bytes 1572864
  424.9 3.8 all-to-all-start.2
  428.9 15.9 %all-to-all-done.2 = bf16[16,2,12288]{2,1,0:T(2,128)(2,1)S(1)} async-done(((bf16[16,2,12288]{2,1,0:T(2,128)(2,1)}), bf16[16,2,12288]{2,1,0:T(2,128)(2,1)S(1)}, u32[]{:S(2)}, u32[]{:S(2)}) %all-to-all-start.2) | async-done | bytes 786464 | tf_op jit(solution)/shard_map/all_to_all | solution.py:141
  444.8 55.2 %reshape.621 = bf16[16384,3,2,4]{3,2,1,0:T(2,128)(2,1)} reshape(bf16[16,2,12288]{2,1,0:T(2,128)(2,1)S(1)} %all-to-all-done.2) | data formatting | bytes 1572864
  500.0 57.2 %copy.87 = bf16[3,2,4,16,1024]{4,2,3,1,0:T(4,128)(2,1)S(1)} copy(bf16[3,2,4,16,1024]{2,1,0,4,3:T(2,128)(2,1)} %bitcast.109) | data formatting | bytes 1572864 | tf_op jit(solution)/shard_map/all_to_all | solution.py:141
  557.4 0.5 convolution_bitcast_fusion.2
  557.8 0.5 convolution_bitcast_fusion.3
  558.3 0.4 fusion.20
  558.7 0.5 convolution_bitcast_fusion.1
  559.2 0.5 convolution_bitcast_fusion
  559.6 0.4 fusion.16
  560.1 0.8 copy.88
  560.9 23.3 %all_to_all.60 = bf16[3,2,64,1024]{3,1,0,2:T(2,128)(2,1)S(1)} all-to-all(bf16[3,2,64,1024]{3,1,0,2:T(2,128)(2,1)S(1)} %copy.88), channel_id=1, replica_groups=mesh['start'=2,'pencil'=16] {'pencil'}, dimensions={2} | all-to-all | bytes 1572864 | tf_op jit(solution)/shard_map/all_to_all | solution.py:165
  584.2 0.4 copy.108
  584.7 0.6 all_to_all.55
  585.3 0.3 fusion.125
  585.5 0.3 reshape_squeeze.6
  585.8 4.6 fusion.23
  590.4 0.3 reshape_squeeze.7
  590.7 4.7 convolution_subtract_fusion
  595.5 1.0 add.441
  (72 shorter events, 3.8 us)
Async XLA Ops:
  0.6 19.9 %copy-start.5 = (s32[2,256]{1,0:T(2,128)S(1)}, s32[2,256]{1,0:T(2,128)}, u32[]{:S(2)}) copy-start(s32[2,256]{1,0:T(2,128)} %param.11) | copy-start | bytes 6148
  1.7 21.2 %collective-permute-start = (bf16[256,256]{1,0:T(8,128)(2,1)S(1)}, bf16[256,256]{1,0:T(8,128)(2,1)S(1)}, u32[]{:S(2)}, u32[]{:S(2)}) collective-permute-start(bf16[256,256]{1,0:T(8,128)(2,1)S(1)} %bitcast.128), channel_id=1, source_target_pairs={{0,2},{1,3},{2,4},{3,5},{4,6},{5,7},{6,8},{7,9},{8,10},{9,11},{10,... | collective-permute-start | bytes 393224 | tf_op jit(solution)/shard_map/ppermute | solution.py:19
  4.7 18.2 %collective-permute-start.1 = (bf16[256,256]{1,0:T(8,128)(2,1)S(1)}, bf16[256,256]{1,0:T(8,128)(2,1)S(1)}, u32[]{:S(2)}, u32[]{:S(2)}) collective-permute-start(bf16[256,256]{1,0:T(8,128)(2,1)S(1)} %bitcast.129), channel_id=1, source_target_pairs={{0,1},{1,2},{2,3},{3,4},{4,5},{5,6},{6,7},{7,8},{8,9},{9,10},{10,1... | collective-permute-start | bytes 393224 | tf_op jit(solution)/shard_map/ppermute | solution.py:19
  6.2 16.7 %collective-permute-start.2 = (bf16[256,256]{1,0:T(8,128)(2,1)S(1)}, bf16[256,256]{1,0:T(8,128)(2,1)S(1)}, u32[]{:S(2)}, u32[]{:S(2)}) collective-permute-start(bf16[256,256]{1,0:T(8,128)(2,1)S(1)} %bitcast.130), channel_id=1, source_target_pairs={{0,15},{1,0},{2,1},{3,2},{4,3},{5,4},{6,5},{7,6},{8,7},{9,8},{10,9... | collective-permute-start | bytes 393224 | tf_op jit(solution)/shard_map/ppermute | solution.py:19
  10.4 12.6 %collective-permute-start.3 = (bf16[256,256]{1,0:T(8,128)(2,1)S(1)}, bf16[256,256]{1,0:T(8,128)(2,1)S(1)}, u32[]{:S(2)}, u32[]{:S(2)}) collective-permute-start(bf16[256,256]{1,0:T(8,128)(2,1)S(1)} %bitcast.131), channel_id=1, source_target_pairs={{0,14},{1,15},{2,0},{3,1},{4,2},{5,3},{6,4},{7,5},{8,6},{9,7},{10,... | collective-permute-start | bytes 393224 | tf_op jit(solution)/shard_map/ppermute | solution.py:19
  28.0 8.6 %collective-permute-start.4 = (bf16[256,256]{1,0:T(8,128)(2,1)S(1)}, bf16[256,256]{1,0:T(8,128)(2,1)S(1)}, u32[]{:S(2)}, u32[]{:S(2)}) collective-permute-start(bf16[256,256]{1,0:T(8,128)(2,1)S(1)} %multiply_reduce_fusion.1), channel_id=1, source_target_pairs={{0,2},{1,3},{2,4},{3,5},{4,6},{5,7},{6,8},{7,9},{8,10},{9,11},{10,... | collective-permute-start | bytes 393224 | tf_op jit(solution)/shard_map/ppermute | solution.py:19
  29.7 8.9 %collective-permute-start.5 = (bf16[256,256]{1,0:T(8,128)(2,1)S(1)}, bf16[256,256]{1,0:T(8,128)(2,1)S(1)}, u32[]{:S(2)}, u32[]{:S(2)}) collective-permute-start(bf16[256,256]{1,0:T(8,128)(2,1)S(1)} %multiply_reduce_fusion.1), channel_id=1, source_target_pairs={{0,1},{1,2},{2,3},{3,4},{4,5},{5,6},{6,7},{7,8},{8,9},{9,10},{10,1... | collective-permute-start | bytes 393224 | tf_op jit(solution)/shard_map/ppermute | solution.py:19
  29.7 9.0 %collective-permute-start.6 = (bf16[256,256]{1,0:T(8,128)(2,1)S(1)}, bf16[256,256]{1,0:T(8,128)(2,1)S(1)}, u32[]{:S(2)}, u32[]{:S(2)}) collective-permute-start(bf16[256,256]{1,0:T(8,128)(2,1)S(1)} %multiply_reduce_fusion.1), channel_id=1, source_target_pairs={{0,15},{1,0},{2,1},{3,2},{4,3},{5,4},{6,5},{7,6},{8,7},{9,8},{10,9... | collective-permute-start | bytes 393224 | tf_op jit(solution)/shard_map/ppermute | solution.py:19
  35.3 6.0 %collective-permute-start.7 = (bf16[256,256]{1,0:T(8,128)(2,1)S(1)}, bf16[256,256]{1,0:T(8,128)(2,1)S(1)}, u32[]{:S(2)}, u32[]{:S(2)}) collective-permute-start(bf16[256,256]{1,0:T(8,128)(2,1)S(1)} %multiply_reduce_fusion.1), channel_id=1, source_target_pairs={{0,14},{1,15},{2,0},{3,1},{4,2},{5,3},{6,4},{7,5},{8,6},{9,7},{10,... | collective-permute-start | bytes 393224 | tf_op jit(solution)/shard_map/ppermute | solution.py:19
  46.5 161.0 %copy-start = (bf16[4,32,512]{2,1,0:T(8,128)(2,1)}, bf16[4,32,512]{2,1,0:T(8,128)(2,1)S(1)}, u32[]{:S(2)}) copy-start(bf16[4,32,512]{2,1,0:T(8,128)(2,1)S(1)} %reshape.589) | copy-start | bytes 393220
  160.1 13.0 %all-to-all-start = ((bf16[16,2,2048]{2,1,0:T(2,128)(2,1)}), bf16[16,2,2048]{2,1,0:T(2,128)(2,1)S(1)}, u32[]{:S(2)}, u32[]{:S(2)}) async-start(bf16[16,2,2048]{2,1,0:T(2,128)(2,1)} %reshape.616), calls=%async_computation | async-start | bytes 262144 | tf_op jit(solution)/shard_map/all_to_all | solution.py:113
  185.4 15.6 %copy-start.3 = (bf16[64,64]{1,0:T(8,128)(2,1)S(1)}, bf16[64,64]{1,0:T(8,128)(2,1)}, u32[]{:S(2)}) copy-start(bf16[64,64]{1,0:T(8,128)(2,1)} %cosine_convert_fusion.3) | copy-start | bytes 24580
  185.4 15.6 %copy-start.4 = (bf16[64,64]{1,0:T(8,128)(2,1)S(1)}, bf16[64,64]{1,0:T(8,128)(2,1)}, u32[]{:S(2)}) copy-start(bf16[64,64]{1,0:T(8,128)(2,1)} %fusion.60) | copy-start | bytes 24580
  201.0 6.5 %copy-start.2 = (bf16[4,32,512]{2,1,0:T(8,128)(2,1)S(1)}, bf16[4,32,512]{2,1,0:T(8,128)(2,1)}, u32[]{:S(2)}) copy-start(bf16[4,32,512]{2,1,0:T(8,128)(2,1)} %param.7) | copy-start | bytes 393220
  203.9 11.3 %all-to-all-start.1 = ((bf16[16,2,2048]{2,1,0:T(2,128)(2,1)}), bf16[16,2,2048]{2,1,0:T(2,128)(2,1)S(1)}, u32[]{:S(2)}, u32[]{:S(2)}) async-start(bf16[16,2,2048]{2,1,0:T(2,128)(2,1)} %reshape.618), calls=%async_computation.1 | async-start | bytes 262144 | tf_op jit(solution)/shard_map/all_to_all | solution.py:126
  424.9 19.9 %all-to-all-start.2 = ((bf16[16,2,12288]{2,1,0:T(2,128)(2,1)}), bf16[16,2,12288]{2,1,0:T(2,128)(2,1)S(1)}, u32[]{:S(2)}, u32[]{:S(2)}) async-start(bf16[16,2,12288]{2,1,0:T(2,128)(2,1)} %reshape.620), calls=%async_computation.2 | async-start | bytes 1572864 | tf_op jit(solution)/shard_map/all_to_all | solution.py:141
  590.7 4.7 copy-start.1
where the time goes:
time: 603 us; the launch traced here: 597 us
  local copies, waits for them, and re-layouts  307 us (51%)
  other arithmetic  177 us (29%)
  waiting for transfers between devices  35.5 us (6%)
  starting transfers between devices  29.8 us (5%)
  blocking collectives  23.3 us (4%)
  matrix products  22.4 us (4%)
    unnamed x3, other arithmetic  163 us
    unnamed x29, local copies, waits for them, and re-layouts  128 us
    another operation x4, local copies, waits for them, and re-layouts, local(): jnp.stack([spec_real.reshape(3, row_count, cell_count), spec_imag.reshape...  79.5 us
    all_to_all x2, local copies, waits for them, and re-layouts, local(): lax.all_to_all(spec_f, 'pencil', split_axis=3, concat_axis=2, tiled=True)  57.3 us
    all_to_all x1, blocking collectives, local(): lax.all_to_all(mixed, 'pencil', split_axis=2, concat_axis=3, tiled=True)  23.3 us
    ppermute x8, starting transfers between devices, shifted(): lax.ppermute(x, axis, [(i, (i + by) % length) for i in range(length)])  17.2 us
    all_to_all x1, waiting for transfers between devices, local(): lax.all_to_all(spec_f, 'pencil', split_axis=3, concat_axis=2, tiled=True)  15.9 us
    all_to_all x2, local copies, waits for them, and re-layouts, local(): lax.all_to_all(flat_warp, 'pencil', split_axis=2, concat_axis=1, tiled=True)  15.5 us
  transfers between devices with their start and end apart: 11, of which 6 were waited for; matrix products, arithmetic and copies ran while one was open for 2% of the time, Pallas kernels for 0%

commit v1 on v0

--- a/solution.py
+++ b/solution.py
@@ -1,8 +1,12 @@
+import functools
 import math
 
 import jax
 import jax.numpy as jnp
+import numpy as np
 from jax import lax
+from jax.experimental import pallas as pl
+from jax.experimental.pallas import tpu as pltpu
 from jax.sharding import PartitionSpec as P
 
 ZB = 2
@@ -52,7 +56,7 @@
     return jnp.dot(onehot, weight_table, precision=lax.Precision.HIGHEST)
 
 
-def local(template, reference_image, velocity, dep_owner, dep_offset, dep_weight):
+def general(template, reference_image, velocity, dep_owner, dep_offset, dep_weight):
     peer_count = lax.axis_size("pencil")
     row_count, plane_count, y_count = template.shape
     full_rows = row_count * peer_count
@@ -173,6 +177,365 @@
     return (warped, gradient)
 
 
+def split_pair(values):
+    high = values.astype(jnp.bfloat16)
+    low = (values - np.asarray(high, np.float64)).astype(jnp.bfloat16)
+    return [high, low]
+
+
+def real_dft(length):
+    half = length // 2
+    waves = np.concatenate([np.arange(half + 1), np.arange(1, half)])
+    angle = 2.0 * np.pi * ((np.arange(length)[:, None] * waves[None, :]) % length) / length
+    table = np.where(np.arange(length)[None, :] <= half, np.cos(angle), np.sin(angle))
+    factor = np.where((waves == 0) | (waves == half), 1.0, 2.0)
+    k = np.where(waves == half, 0, waves) * (2.0 * np.pi / length)
+    return table, (table * factor[None, :]).T, k
+
+
+def derivative(length):
+    series = np.arange(length)
+    angle = 2.0 * np.pi * ((series[:, None] * series[None, :]) % length) / length
+    cos, sin = np.cos(angle), np.sin(angle)
+    k = np.where(series < length // 2, series, series - length)
+    k = np.where(series == length // 2, 0, k) * (2.0 * np.pi / length)
+    return ((sin * k) @ cos - (cos * k) @ sin) / length
+
+
+@functools.lru_cache(None)
+def tables(n, rows, planes, ny):
+    nx = n * rows
+    m = nx * ZB
+    index = np.arange(m)
+    line_x = index // (ZB * rows) * rows + index % rows
+    line_z = index // rows % ZB
+    wide = np.arange(2 * m)
+    wide_dev = wide // (2 * ZB * rows)
+    wide_half = wide // (ZB * rows) % 2
+    wide_z = wide // rows % ZB
+    wide_row = wide % rows
+    slab = wide_half * m + wide_row * planes + wide_dev * ZB + wide_z
+    line = wide_half * m + wide_dev * (ZB * rows) + wide_z * rows + wide_row
+    eye = np.eye(2 * m)
+    to_message = eye[slab]
+    from_message = eye[slab].T
+    line_message = eye[line]
+    line_second = eye[line].T[m:]
+    wide_x = np.where(wide_half == 0, wide_dev * rows + wide_row, 8 * nx)
+    first_x = np.where(line_z[:, None] == wide_z[None, :], wide_x[None, :], 8 * nx)
+    second_x = np.where(line_z[:, None] == line_z[None, :], line_x[None, :], 8 * nx)
+    same_z = line_z[:, None] == line_z[None, :]
+    dx = derivative(nx)[line_x[None, :], line_x[:, None]] * same_z
+    dy = derivative(ny)
+    plane_last = np.zeros((nx, m))
+    plane_first = np.zeros((nx, m))
+    plane_last[line_x[line_z == ZB - 1], index[line_z == ZB - 1]] = 1.0
+    plane_first[line_x[line_z == 0], index[line_z == 0]] = 1.0
+    dz = np.zeros((m, 2 * m))
+    for r in range(m):
+        x, z = line_x[r], line_z[r]
+        for step, sign in ((1, 0.5), (-1, -0.5)):
+            if z + step < 0:
+                column = m + x
+            elif z + step >= ZB:
+                column = m + nx + x
+            else:
+                column = int(np.nonzero((line_x == x) & (line_z == z + step))[0][0])
+            dz[r, column] += sign
+    fx, bx, kx = real_dft(nx)
+    fy, by, ky = real_dft(ny)
+    out_z = index // nx
+    out_k = index % nx
+    forward = fx.T[out_k][:, line_x] * (out_z[:, None] == line_z[None, :])
+    backward = bx.T[line_x][:, out_k] * (line_z[:, None] == out_z[None, :])
+    gain = force_gain / (
+        nx * ny * (1.0 + h1_weight * (kx[out_k][:, None] ** 2 + ky[None, :] ** 2))
+    )
+    per = ny // SEG
+    groups = planes // ZB
+    lanes = np.arange(rows * groups * per)
+    lane_row = lanes // (groups * per)
+    lane_group = lanes // per % groups
+    code_mask = (lane_group[None, :] == (index // (ZB * rows))[:, None]) & (
+        lane_row[None, :] == (index % rows)[:, None]
+    )
+    code_spread = np.zeros((4, lanes.size, 128))
+    for j in range(4):
+        code_spread[j, lanes, j * per + lanes % per] = 1.0
+    b16 = lambda t: np.asarray(t, np.float64).astype(jnp.bfloat16)
+    f32 = lambda t: np.asarray(t, np.float32)
+    return (
+        b16(to_message),
+        b16(from_message),
+        b16(line_message),
+        b16(line_second),
+        f32(first_x),
+        f32(second_x),
+        *split_pair(dx),
+        *split_pair(dy),
+        b16(np.concatenate([plane_last, plane_first])),
+        b16(dz),
+        b16(forward),
+        b16(backward),
+        b16(fy),
+        b16(by),
+        f32(gain),
+        b16(code_mask),
+        b16(code_spread),
+    )
+
+
+def dot(a, b):
+    return jnp.dot(a, b, preferred_element_type=jnp.float32)
+
+
+def body(
+    n,
+    template_ref,
+    image_ref,
+    velocity_ref,
+    code_ref,
+    to_message,
+    from_message,
+    line_message,
+    line_second,
+    first_x,
+    second_x,
+    dx_high,
+    dx_low,
+    dy_high,
+    dy_low,
+    planes_out,
+    dz,
+    forward_x,
+    backward_x,
+    forward_y,
+    backward_y,
+    gain,
+    code_mask,
+    code_spread,
+    warped_ref,
+    gradient_ref,
+    code_send,
+    code_recv,
+    image_send,
+    image_recv,
+    halo_send,
+    halo_recv,
+    back_send,
+    back_recv,
+    code_sems,
+    image_sems,
+    halo_sems,
+    back_sems,
+):
+    me = lax.axis_index("pencil")
+    rows, planes, ny = template_ref.shape
+    m = n * rows * ZB
+    nx = n * rows
+    per = ny // SEG
+    half = ny // 2
+    after = lax.rem(me + 1, n)
+    before = lax.rem(me + n - 1, n)
+
+    barrier = pltpu.get_barrier_semaphore()
+
+    def greet(off, carry):
+        pl.semaphore_signal(
+            barrier,
+            inc=1,
+            device_id={"pencil": lax.rem(me + off, n)},
+            device_id_type=pl.DeviceIdType.MESH,
+        )
+        return carry
+
+    lax.fori_loop(1, n, greet, 0)
+
+    def copy(send, recv, sems, off, slot):
+        return pltpu.make_async_remote_copy(
+            src_ref=send.at[lax.rem(me + off, n)],
+            dst_ref=recv.at[slot],
+            send_sem=sems.at[0, off],
+            recv_sem=sems.at[1, off],
+            device_id={"pencil": lax.rem(me + off, n)},
+            device_id_type=pl.DeviceIdType.MESH,
+        )
+
+    def scatter(send, recv, sems):
+        def step(off, carry):
+            copy(send, recv, sems, off, me).start()
+            return carry
+
+        lax.fori_loop(1, n, step, 0)
+        recv[me] = send[me]
+
+    def collect(send, recv, sems):
+        def step(off, carry):
+            copy(send, recv, sems, off, lax.rem(me + n - off, n)).wait_recv()
+            return carry
+
+        lax.fori_loop(1, n, step, 0)
+
+    def drain(send, recv, sems):
+        def step(off, carry):
+            copy(send, recv, sems, off, me).wait_send()
+            return carry
+
+        lax.fori_loop(1, n, step, 0)
+
+    codes = jnp.zeros((m, 128), jnp.float32)
+    for j in range(4):
+        codes += dot(code_mask[...] * code_ref[j : j + 1, :], code_spread[j])
+    code_send[...] = codes.reshape(n, ZB * rows, 128)
+    both = jnp.concatenate(
+        [template_ref[...].reshape(m, ny), image_ref[...].reshape(m, ny)], axis=0
+    )
+    image_send[...] = (
+        dot(to_message[...], both).astype(jnp.bfloat16).reshape(n, 2 * ZB * rows, ny)
+    )
+    pl.semaphore_wait(barrier, n - 1)
+    scatter(code_send, code_recv, code_sems)
+    scatter(image_send, image_recv, image_sems)
+
+    collect(code_send, code_recv, code_sems)
+    code = code_recv[...].reshape(m, 128)
+    t = (code + 0.5) / Q
+    weights = (
+        -t * (t - 1.0) * (t - 2.0) / 6.0,
+        (t + 1.0) * (t - 1.0) * (t - 2.0) / 2.0,
+        -(t + 1.0) * t * (t - 2.0) / 2.0,
+        (t + 1.0) * t * (t - 1.0) / 6.0,
+    )
+
+    def stencil(section, group, place):
+        at = section * per + group
+        delta = place - code[:, at : at + 1]
+        delta = jnp.where(delta < 0.0, delta + nx, delta)
+        at = 2 * per + at
+        taps = jnp.zeros_like(delta)
+        for k in range(4):
+            taps = jnp.where(delta == float(k), weights[k][:, at : at + 1], taps)
+        high = taps.astype(jnp.bfloat16)
+        low = (taps - high.astype(jnp.float32)).astype(jnp.bfloat16)
+        return high, low
+
+    first = [stencil(0, g, first_x[...]) for g in range(per)]
+    collect(image_send, image_recv, image_sems)
+    images = image_recv[...].reshape(2 * m, ny)
+    warped = []
+    for g in range(per):
+        high, low = first[g]
+        seg = images[:, g * SEG : (g + 1) * SEG]
+        seg = (dot(high, seg) + dot(low, seg)).astype(jnp.bfloat16)
+        high, low = stencil(1, g, second_x[...])
+        warped.append((dot(high, seg) + dot(low, seg)).astype(jnp.bfloat16))
+    warped = jnp.concatenate(warped, axis=1)
+
+    halo_send[...] = dot(planes_out[...], warped).astype(jnp.bfloat16).reshape(2, nx, ny)
+    halos = [
+        pltpu.make_async_remote_copy(
+            src_ref=halo_send.at[side],
+            dst_ref=halo_recv.at[side],
+            send_sem=halo_sems.at[0, side],
+            recv_sem=halo_sems.at[1, side],
+            device_id={"pencil": (after, before)[side]},
+            device_id_type=pl.DeviceIdType.MESH,
+        )
+        for side in range(2)
+    ]
+    for halo in halos:
+        halo.start()
+
+    def send_back(slot, value):
+        stacked = jnp.concatenate([value[:, :half], value[:, half:]], axis=0)
+        message = dot(line_message[...], stacked).astype(jnp.bfloat16)
+        back_send[slot] = message.reshape(n, 2 * ZB * rows, half)
+        scatter(back_send.at[slot], back_recv.at[slot], back_sems.at[slot])
+
+    send_back(0, warped)
+    residual = dot(line_second[...], images) - warped.astype(jnp.float32)
+
+    def smooth(slot, slope):
+        force = (slope * residual).astype(jnp.bfloat16)
+        spectrum = dot(force, forward_y[...]).astype(jnp.bfloat16)
+        spectrum = (dot(forward_x[...], spectrum) * gain[...]).astype(jnp.bfloat16)
+        spectrum = dot(backward_x[...], spectrum).astype(jnp.bfloat16)
+        send_back(slot, dot(spectrum, backward_y[...]).astype(jnp.bfloat16))
+
+    smooth(1, dot(dx_high[...], warped) + dot(dx_low[...], warped))
+    smooth(2, dot(warped, dy_high[...]) + dot(warped, dy_low[...]))
+    for halo in halos:
+        halo.wait_recv()
+    smooth(
+        3, dot(dz[...], jnp.concatenate([warped, halo_recv[0], halo_recv[1]], axis=0))
+    )
+
+    for slot in range(4):
+        collect(back_send.at[slot], back_recv.at[slot], back_sems.at[slot])
+        home = dot(from_message[...], back_recv[slot].reshape(2 * m, half))
+        home = jnp.concatenate([home[:m], home[m:]], axis=1).reshape(rows, planes, ny)
+        if slot == 0:
+            warped_ref[...] = home.astype(jnp.bfloat16)
+        else:
+            gradient_ref[slot - 1] = velocity_ref[slot - 1] + home
+
+    drain(code_send, code_recv, code_sems)
+    drain(image_send, image_recv, image_sems)
+    for halo in halos:
+        halo.wait_send()
+    for slot in range(4):
+        drain(back_send.at[slot], back_recv.at[slot], back_sems.at[slot])
+
+
+def by_groups(template, reference_image, velocity, dep_owner, dep_offset, dep_weight):
+    n = lax.axis_size("pencil")
+    rows, planes, ny = template.shape
+    per_row = planes // ZB * (ny // SEG)
+    m = n * rows * ZB
+    base = (dep_owner * rows + dep_offset // per_row) % (n * rows)
+    codes = jnp.concatenate([base, dep_weight], axis=0).astype(jnp.bfloat16)
+    constants = [jnp.asarray(t) for t in tables(n, rows, planes, ny)]
+    vmem = pl.BlockSpec(memory_space=pltpu.VMEM)
+    b16, f32 = jnp.bfloat16, jnp.float32
+    return pl.pallas_call(
+        functools.partial(body, n),
+        out_shape=(
+            jax.ShapeDtypeStruct(template.shape, b16),
+            jax.ShapeDtypeStruct(velocity.shape, f32),
+        ),
+        in_specs=[vmem] * (4 + len(constants)),
+        out_specs=(vmem, vmem),
+        scratch_shapes=[
+            pltpu.VMEM((n, ZB * rows, 128), f32),
+            pltpu.VMEM((n, ZB * rows, 128), f32),
+            pltpu.VMEM((n, 2 * ZB * rows, ny), b16),
+            pltpu.VMEM((n, 2 * ZB * rows, ny), b16),
+            pltpu.VMEM((2, n * rows, ny), b16),
+            pltpu.VMEM((2, n * rows, ny), b16),
+            pltpu.VMEM((4, n, 2 * ZB * rows, ny // 2), b16),
+            pltpu.VMEM((4, n, 2 * ZB * rows, ny // 2), b16),
+            pltpu.SemaphoreType.DMA((2, n)),
+            pltpu.SemaphoreType.DMA((2, n)),
+            pltpu.SemaphoreType.DMA((2, 2)),
+            pltpu.SemaphoreType.DMA((4, 2, n)),
+        ],
+        compiler_params=pltpu.CompilerParams(
+            collective_id=0, has_side_effects=True, vmem_limit_bytes=40 * 1024 * 1024
+        ),
+        cost_estimate=pl.CostEstimate(
+            flops=24 * m * ny * ny, bytes_accessed=8 * m * ny * 4, transcendentals=0
+        ),
+    )(template, reference_image, velocity, codes, *constants)
+
+
+def local(template, *others):
+    n = lax.axis_size("pencil")
+    rows, planes, _ = template.shape
+    if n > 2 and planes == n * ZB and rows * ZB == 8 and n * rows <= 256:
+        return by_groups(template, *others)
+    return general(template, *others)
+
+
 def solution(mesh):
     in_specs = (
         P("pencil", "start", None),

time: 603 us -> 55.7 us (0.09)
  local copies, waits for them, and re-layouts: 307 us -> 20.5 us
  other arithmetic: 177 us -> 1.42 us
  waiting for transfers between devices: 35.5 us -> 0 us
  Pallas kernels: 0 us -> 32 us
  starting transfers between devices: 29.8 us -> 0 us
  blocking collectives: 23.3 us -> 0 us
  matrix products: 22.4 us -> 0 us
    unnamed x3 -> x0, other arithmetic: 163 us -> none
    unnamed x29 -> x46, local copies, waits for them, and re-layouts: 128 us -> 20.5 us
    another operation x10 -> x0, local copies, waits for them, and re-layouts: 94 us -> none  [the longest x4 79.5 us: local(): jnp.stack([spec_real.reshape(3, row_count, cell_count), spec_imag.reshape...]
    all_to_all x6 -> x0, local copies, waits for them, and re-layouts: 73.9 us -> none  [the longest x2 57.3 us: local(): lax.all_to_all(spec_f, 'pencil', split_axis=3, concat_axis=2, tiled=True)]
    pallas_call x0 -> x1, Pallas kernels: none -> 32 us  [by_groups(): pl.pallas_call(functools.partial(body, n), out_shape=(jax.ShapeDtypeStruc...]
    all_to_all x3 -> x0, waiting for transfers between devices: 30.5 us -> none  [the longest x1 15.9 us: local(): lax.all_to_all(spec_f, 'pencil', split_axis=3, concat_axis=2, tiled=True)]
    all_to_all x1 -> x0, blocking collectives: 23.3 us -> none  [local(): lax.all_to_all(mixed, 'pencil', split_axis=2, concat_axis=3, tiled=True)]
    dot_general x14 -> x0, matrix products: 22.4 us -> none  [the longest x1 4.88 us: local(): jnp.dot(force_lines, -sin_y, preferred_element_type=jnp.float32)]
  transfers between devices with their start and end apart: 11 -> 0, of which waited for: 6 -> 0; matrix products, arithmetic and copies ran while one was open for 2% -> 0% of each run, Pallas kernels for 0% -> 0%
where the time goes in v1:
time: 55.7 us; the launch traced here: 54.6 us
  Pallas kernels  32 us (57%)
  local copies, waits for them, and re-layouts  20.5 us (37%)
  other arithmetic  1.42 us (3%)
  between operations  0.69 us (1%)
    pallas_call x1, Pallas kernels, by_groups(): pl.pallas_call(functools.partial(body, n), out_shape=(jax.ShapeDtypeStruc...  32 us
    unnamed x46, local copies, waits for them, and re-layouts  20.5 us
    another operation x2, other arithmetic  1.41 us

profile of v1, /device:TPU:0, one launch (start us, length us, event | category | flops | bytes accessed | tf_op | source)
XLA Modules:
  0.0 54.6 jit_solution(5159528421399233815)
XLA Ops:
  0.6 0.0 copy-start.17
  0.6 0.7 %fusion.1 = bf16[2,256]{1,0:T(2,128)(2,1)S(1)} fusion(s32[2,256]{1,0:T(2,128)} %param.29, s32[2,256]{1,0:T(2,128)} %param.28), kind=kLoop, calls=%fused_computation.9 | loop fusion | flops 14848 | bytes 5120 | tf_op jit(solution)/shard_map/convert
  1.4 0.7 %convert.7 = bf16[2,256]{1,0:T(2,128)(2,1)S(1)} convert(s32[2,256]{1,0:T(2,128)} %param.30) | non-fusion elementwise | flops 512 | bytes 3072 | tf_op jit(solution)/shard_map/convert.1
  2.1 0.0 copy-done.17
  2.1 0.0 copy-start
  2.1 1.1 %copy-done = f32[3,4,32,512]{3,2,1,0:T(8,128)S(1)} copy-done((f32[3,4,32,512]{3,2,1,0:T(8,128)S(1)}, f32[3,4,32,512]{3,2,1,0:T(8,128)}, u32[]{:S(2)}) %copy-start) | copy-done | bytes 786456
  3.2 0.0 copy-start.1
  3.2 1.0 %copy-done.1 = bf16[512,512]{1,0:T(8,128)(2,1)S(1)} copy-done((bf16[512,512]{1,0:T(8,128)(2,1)S(1)}, bf16[512,512]{1,0:T(8,128)(2,1)}, u32[]{:S(2)}) %copy-start.1) | copy-done | bytes 524312
  4.3 0.0 copy-start.2
  4.3 1.0 %copy-done.2 = bf16[512,512]{1,0:T(8,128)(2,1)S(1)} copy-done((bf16[512,512]{1,0:T(8,128)(2,1)S(1)}, bf16[512,512]{1,0:T(8,128)(2,1)}, u32[]{:S(2)}) %copy-start.2) | copy-done | bytes 524312
  5.3 0.0 copy-start.3
  5.3 1.0 %copy-done.3 = bf16[512,512]{1,0:T(8,128)(2,1)S(1)} copy-done((bf16[512,512]{1,0:T(8,128)(2,1)S(1)}, bf16[512,512]{1,0:T(8,128)(2,1)}, u32[]{:S(2)}) %copy-start.3) | copy-done | bytes 524312
  6.3 0.0 copy-start.4
  6.3 1.0 %copy-done.4 = bf16[512,512]{1,0:T(8,128)(2,1)S(1)} copy-done((bf16[512,512]{1,0:T(8,128)(2,1)S(1)}, bf16[512,512]{1,0:T(8,128)(2,1)}, u32[]{:S(2)}) %copy-start.4) | copy-done | bytes 524312
  7.4 0.0 copy-start.5
  7.4 0.9 %copy-done.5 = bf16[4,256,128]{2,1,0:T(8,128)(2,1)S(1)} copy-done((bf16[4,256,128]{2,1,0:T(8,128)(2,1)S(1)}, bf16[4,256,128]{2,1,0:T(8,128)(2,1)}, u32[]{:S(2)}) %copy-start.5) | copy-done | bytes 262168
  8.3 0.0 copy-start.6
  8.3 0.9 %copy-done.6 = f32[128,512]{1,0:T(8,128)S(1)} copy-done((f32[128,512]{1,0:T(8,128)S(1)}, f32[128,512]{1,0:T(8,128)}, u32[]{:S(2)}) %copy-start.6) | copy-done | bytes 262168
  9.3 0.0 copy-start.7
  9.3 0.9 %copy-done.7 = bf16[4,32,512]{2,1,0:T(8,128)(2,1)S(1)} copy-done((bf16[4,32,512]{2,1,0:T(8,128)(2,1)S(1)}, bf16[4,32,512]{2,1,0:T(8,128)(2,1)}, u32[]{:S(2)}) %copy-start.7) | copy-done | bytes 131096
  10.2 0.0 copy-start.8
  10.2 0.9 %copy-done.8 = bf16[4,32,512]{2,1,0:T(8,128)(2,1)S(1)} copy-done((bf16[4,32,512]{2,1,0:T(8,128)(2,1)S(1)}, bf16[4,32,512]{2,1,0:T(8,128)(2,1)}, u32[]{:S(2)}) %copy-start.8) | copy-done | bytes 131096
  11.1 0.0 copy-start.9
  11.1 0.9 %copy-done.9 = f32[128,256]{1,0:T(8,128)S(1)} copy-done((f32[128,256]{1,0:T(8,128)S(1)}, f32[128,256]{1,0:T(8,128)}, u32[]{:S(2)}) %copy-start.9) | copy-done | bytes 131096
  12.0 0.0 copy-start.10
  12.0 0.9 %copy-done.10 = bf16[256,256]{1,0:T(8,128)(2,1)S(1)} copy-done((bf16[256,256]{1,0:T(8,128)(2,1)S(1)}, bf16[256,256]{1,0:T(8,128)(2,1)}, u32[]{:S(2)}) %copy-start.10) | copy-done | bytes 131096
  12.9 0.0 copy-start.11
  12.9 0.9 %copy-done.11 = bf16[256,256]{1,0:T(8,128)(2,1)S(1)} copy-done((bf16[256,256]{1,0:T(8,128)(2,1)S(1)}, bf16[256,256]{1,0:T(8,128)(2,1)}, u32[]{:S(2)}) %copy-start.11) | copy-done | bytes 131096
  13.8 0.0 copy-start.12
  13.8 0.9 %copy-done.12 = bf16[256,256]{1,0:T(8,128)(2,1)S(1)} copy-done((bf16[256,256]{1,0:T(8,128)(2,1)S(1)}, bf16[256,256]{1,0:T(8,128)(2,1)}, u32[]{:S(2)}) %copy-start.12) | copy-done | bytes 131096
  14.7 0.0 copy-start.13
  14.7 0.8 %copy-done.13 = bf16[128,256]{1,0:T(8,128)(2,1)S(1)} copy-done((bf16[128,256]{1,0:T(8,128)(2,1)S(1)}, bf16[128,256]{1,0:T(8,128)(2,1)}, u32[]{:S(2)}) %copy-start.13) | copy-done | bytes 65560
  15.6 0.0 copy-start.14
  15.6 0.8 %copy-done.14 = bf16[128,256]{1,0:T(8,128)(2,1)S(1)} copy-done((bf16[128,256]{1,0:T(8,128)(2,1)S(1)}, bf16[128,256]{1,0:T(8,128)(2,1)}, u32[]{:S(2)}) %copy-start.14) | copy-done | bytes 65560
  16.4 0.0 copy-start.15
  16.4 0.8 %copy-done.15 = f32[128,128]{1,0:T(8,128)S(1)} copy-done((f32[128,128]{1,0:T(8,128)S(1)}, f32[128,128]{1,0:T(8,128)}, u32[]{:S(2)}) %copy-start.15) | copy-done | bytes 65560
  17.2 0.0 copy-start.16
  17.2 0.8 %copy-done.16 = bf16[128,256]{1,0:T(8,128)(2,1)S(1)} copy-done((bf16[128,256]{1,0:T(8,128)(2,1)S(1)}, bf16[128,256]{1,0:T(8,128)(2,1)}, u32[]{:S(2)}) %copy-start.16) | copy-done | bytes 65560
  18.1 0.0 copy-start.18
  18.1 0.8 %copy-done.18 = bf16[128,128]{1,0:T(8,128)(2,1)S(1)} copy-done((bf16[128,128]{1,0:T(8,128)(2,1)S(1)}, bf16[128,128]{1,0:T(8,128)(2,1)}, u32[]{:S(2)}) %copy-start.18) | copy-done | bytes 32792
  18.8 0.0 copy-start.19
  18.8 0.8 %copy-done.19 = bf16[128,128]{1,0:T(8,128)(2,1)S(1)} copy-done((bf16[128,128]{1,0:T(8,128)(2,1)S(1)}, bf16[128,128]{1,0:T(8,128)(2,1)}, u32[]{:S(2)}) %copy-start.19) | copy-done | bytes 32792
  19.6 0.0 copy-start.20
  19.6 0.8 %copy-done.20 = bf16[128,128]{1,0:T(8,128)(2,1)S(1)} copy-done((bf16[128,128]{1,0:T(8,128)(2,1)S(1)}, bf16[128,128]{1,0:T(8,128)(2,1)}, u32[]{:S(2)}) %copy-start.20) | copy-done | bytes 32792
  20.3 0.0 copy-start.21
  20.3 0.8 %copy-done.21 = bf16[128,128]{1,0:T(8,128)(2,1)S(1)} copy-done((bf16[128,128]{1,0:T(8,128)(2,1)S(1)}, bf16[128,128]{1,0:T(8,128)(2,1)}, u32[]{:S(2)}) %copy-start.21) | copy-done | bytes 32792
  21.1 32.0 %shard_map.248 = (bf16[4,32,512]{2,1,0:T(8,128)(2,1)S(1)}, f32[3,4,32,512]{3,2,1,0:T(8,128)S(1)}) custom-call(bf16[4,32,512]{2,1,0:T(8,128)(2,1)S(1)} %copy-done.7, bf16[4,32,512]{2,1,0:T(8,128)(2,1)S(1)} %copy-done.8, f32[3,4,32,512]{3,2,1,0:T(8,128)S(1)} %copy-done, bf16[4,256]{1,0:T(4,128)(2,1)S(1)} %pad_maximum_fusion.code_ref, ...), custom_call_target="tpu_custom_call" | custom-call | flops 805306368 | bytes 2097152 | tf_op jit(solution)/shard_map/pallas_call | solution.py:500
  53.1 0.7 %copy.29 = bf16[4,32,512]{2,1,0:T(8,128)(2,1)} copy(bf16[4,32,512]{2,1,0:T(8,128)(2,1)S(1)} %get-tuple-element.4) | data formatting | bytes 262144
  53.8 0.9 %copy.30 = f32[3,4,32,512]{3,2,1,0:T(8,128)} copy(f32[3,4,32,512]{3,2,1,0:T(8,128)S(1)} %get-tuple-element.5) | data formatting | bytes 1572864
  (1 shorter events, 0.0 us)
Async XLA Ops:
  0.6 1.4 %copy-start.17 = (bf16[128,128]{1,0:T(8,128)(2,1)S(1)}, bf16[128,128]{1,0:T(8,128)(2,1)}, u32[]{:S(2)}) copy-start(bf16[128,128]{1,0:T(8,128)(2,1)} %constant.81.clone.backward_x) | copy-start | bytes 98308
  2.1 1.1 %copy-start = (f32[3,4,32,512]{3,2,1,0:T(8,128)S(1)}, f32[3,4,32,512]{3,2,1,0:T(8,128)}, u32[]{:S(2)}) copy-start(f32[3,4,32,512]{3,2,1,0:T(8,128)} %velocity_ref.1) | copy-start | bytes 2359300
  3.2 1.0 %copy-start.1 = (bf16[512,512]{1,0:T(8,128)(2,1)S(1)}, bf16[512,512]{1,0:T(8,128)(2,1)}, u32[]{:S(2)}) copy-start(bf16[512,512]{1,0:T(8,128)(2,1)} %constant.83.clone.backward_y) | copy-start | bytes 1572868
  4.3 1.0 %copy-start.2 = (bf16[512,512]{1,0:T(8,128)(2,1)S(1)}, bf16[512,512]{1,0:T(8,128)(2,1)}, u32[]{:S(2)}) copy-start(bf16[512,512]{1,0:T(8,128)(2,1)} %constant.82.clone.forward_y) | copy-start | bytes 1572868
  5.3 1.0 %copy-start.3 = (bf16[512,512]{1,0:T(8,128)(2,1)S(1)}, bf16[512,512]{1,0:T(8,128)(2,1)}, u32[]{:S(2)}) copy-start(bf16[512,512]{1,0:T(8,128)(2,1)} %constant.77.clone.dy_low) | copy-start | bytes 1572868
  6.3 1.0 %copy-start.4 = (bf16[512,512]{1,0:T(8,128)(2,1)S(1)}, bf16[512,512]{1,0:T(8,128)(2,1)}, u32[]{:S(2)}) copy-start(bf16[512,512]{1,0:T(8,128)(2,1)} %constant.76.clone.dy_high) | copy-start | bytes 1572868
  7.4 0.9 %copy-start.5 = (bf16[4,256,128]{2,1,0:T(8,128)(2,1)S(1)}, bf16[4,256,128]{2,1,0:T(8,128)(2,1)}, u32[]{:S(2)}) copy-start(bf16[4,256,128]{2,1,0:T(8,128)(2,1)} %constant.86.clone.code_spread) | copy-start | bytes 786436
  8.3 0.9 %copy-start.6 = (f32[128,512]{1,0:T(8,128)S(1)}, f32[128,512]{1,0:T(8,128)}, u32[]{:S(2)}) copy-start(f32[128,512]{1,0:T(8,128)} %constant.84.clone.gain) | copy-start | bytes 786436
  9.3 0.9 %copy-start.7 = (bf16[4,32,512]{2,1,0:T(8,128)(2,1)S(1)}, bf16[4,32,512]{2,1,0:T(8,128)(2,1)}, u32[]{:S(2)}) copy-start(bf16[4,32,512]{2,1,0:T(8,128)(2,1)} %template_ref.1) | copy-start | bytes 393220
  10.2 0.9 %copy-start.8 = (bf16[4,32,512]{2,1,0:T(8,128)(2,1)S(1)}, bf16[4,32,512]{2,1,0:T(8,128)(2,1)}, u32[]{:S(2)}) copy-start(bf16[4,32,512]{2,1,0:T(8,128)(2,1)} %image_ref.1) | copy-start | bytes 393220
  11.1 0.9 %copy-start.9 = (f32[128,256]{1,0:T(8,128)S(1)}, f32[128,256]{1,0:T(8,128)}, u32[]{:S(2)}) copy-start(f32[128,256]{1,0:T(8,128)} %constant.72.clone.first_x) | copy-start | bytes 393220
  12.0 0.9 %copy-start.10 = (bf16[256,256]{1,0:T(8,128)(2,1)S(1)}, bf16[256,256]{1,0:T(8,128)(2,1)}, u32[]{:S(2)}) copy-start(bf16[256,256]{1,0:T(8,128)(2,1)} %constant.70.clone.line_message) | copy-start | bytes 393220
  12.9 0.9 %copy-start.11 = (bf16[256,256]{1,0:T(8,128)(2,1)S(1)}, bf16[256,256]{1,0:T(8,128)(2,1)}, u32[]{:S(2)}) copy-start(bf16[256,256]{1,0:T(8,128)(2,1)} %constant.69.clone.from_message) | copy-start | bytes 393220
  13.8 0.9 %copy-start.12 = (bf16[256,256]{1,0:T(8,128)(2,1)S(1)}, bf16[256,256]{1,0:T(8,128)(2,1)}, u32[]{:S(2)}) copy-start(bf16[256,256]{1,0:T(8,128)(2,1)} %constant.68.clone.to_message) | copy-start | bytes 393220
  14.7 0.8 %copy-start.13 = (bf16[128,256]{1,0:T(8,128)(2,1)S(1)}, bf16[128,256]{1,0:T(8,128)(2,1)}, u32[]{:S(2)}) copy-start(bf16[128,256]{1,0:T(8,128)(2,1)} %constant.85.clone.code_mask) | copy-start | bytes 196612
  15.6 0.8 %copy-start.14 = (bf16[128,256]{1,0:T(8,128)(2,1)S(1)}, bf16[128,256]{1,0:T(8,128)(2,1)}, u32[]{:S(2)}) copy-start(bf16[128,256]{1,0:T(8,128)(2,1)} %constant.79.clone.dz) | copy-start | bytes 196612
  16.4 0.8 %copy-start.15 = (f32[128,128]{1,0:T(8,128)S(1)}, f32[128,128]{1,0:T(8,128)}, u32[]{:S(2)}) copy-start(f32[128,128]{1,0:T(8,128)} %constant.73.clone.second_x) | copy-start | bytes 196612
  17.2 0.8 %copy-start.16 = (bf16[128,256]{1,0:T(8,128)(2,1)S(1)}, bf16[128,256]{1,0:T(8,128)(2,1)}, u32[]{:S(2)}) copy-start(bf16[128,256]{1,0:T(8,128)(2,1)} %constant.71.clone.line_second) | copy-start | bytes 196612
  18.1 0.8 %copy-start.18 = (bf16[128,128]{1,0:T(8,128)(2,1)S(1)}, bf16[128,128]{1,0:T(8,128)(2,1)}, u32[]{:S(2)}) copy-start(bf16[128,128]{1,0:T(8,128)(2,1)} %constant.80.clone.forward_x) | copy-start | bytes 98308
  18.8 0.8 %copy-start.19 = (bf16[128,128]{1,0:T(8,128)(2,1)S(1)}, bf16[128,128]{1,0:T(8,128)(2,1)}, u32[]{:S(2)}) copy-start(bf16[128,128]{1,0:T(8,128)(2,1)} %constant.78.clone.planes_out) | copy-start | bytes 98308
  19.6 0.8 %copy-start.20 = (bf16[128,128]{1,0:T(8,128)(2,1)S(1)}, bf16[128,128]{1,0:T(8,128)(2,1)}, u32[]{:S(2)}) copy-start(bf16[128,128]{1,0:T(8,128)(2,1)} %constant.75.clone.dx_low) | copy-start | bytes 98308
  20.3 0.8 %copy-start.21 = (bf16[128,128]{1,0:T(8,128)(2,1)S(1)}, bf16[128,128]{1,0:T(8,128)(2,1)}, u32[]{:S(2)}) copy-start(bf16[128,128]{1,0:T(8,128)(2,1)} %constant.74.clone.dx_high) | copy-start | bytes 98308

commit v2 on v1

--- a/solution.py
+++ b/solution.py
@@ -220,9 +220,15 @@
     to_message = eye[slab]
     from_message = eye[slab].T
     line_message = eye[line]
-    line_second = eye[line].T[m:]
-    wide_x = np.where(wide_half == 0, wide_dev * rows + wide_row, 8 * nx)
-    first_x = np.where(line_z[:, None] == wide_z[None, :], wide_x[None, :], 8 * nx)
+    wide_x = wide_dev * rows + wide_row
+    first_x = [
+        np.where(
+            (line_z[:, None] == wide_z[None, :]) & (wide_half == h)[None, :],
+            wide_x[None, :],
+            8 * nx,
+        )
+        for h in range(2)
+    ]
     second_x = np.where(line_z[:, None] == line_z[None, :], line_x[None, :], 8 * nx)
     same_z = line_z[:, None] == line_z[None, :]
     dx = derivative(nx)[line_x[None, :], line_x[:, None]] * same_z
@@ -264,71 +270,63 @@
         code_spread[j, lanes, j * per + lanes % per] = 1.0
     b16 = lambda t: np.asarray(t, np.float64).astype(jnp.bfloat16)
     f32 = lambda t: np.asarray(t, np.float32)
-    return (
-        b16(to_message),
-        b16(from_message),
-        b16(line_message),
-        b16(line_second),
-        f32(first_x),
-        f32(second_x),
-        *split_pair(dx),
-        *split_pair(dy),
-        b16(np.concatenate([plane_last, plane_first])),
-        b16(dz),
-        b16(forward),
-        b16(backward),
-        b16(fy),
-        b16(by),
-        f32(gain),
-        b16(code_mask),
-        b16(code_spread),
-    )
+    return {
+        "early": b16(np.concatenate([to_message, code_mask])),
+        "spread": b16(code_spread),
+        "first": f32(first_x),
+        "second": f32(second_x),
+        "lines": b16(np.concatenate([line_message, line_message.T, to_message.T, dz])),
+        "ends": b16(np.concatenate([plane_last, plane_first])),
+        "dx": np.concatenate([*split_pair(dx)]),
+        "dy": np.concatenate([*split_pair(dy)]),
+        "x": b16(np.concatenate([forward, backward])),
+        "fy": b16(fy),
+        "by": b16(by),
+        "gain": f32(gain),
+    }
 
 
 def dot(a, b):
     return jnp.dot(a, b, preferred_element_type=jnp.float32)
 
 
-def body(
-    n,
-    template_ref,
-    image_ref,
-    velocity_ref,
-    code_ref,
-    to_message,
-    from_message,
-    line_message,
-    line_second,
-    first_x,
-    second_x,
-    dx_high,
-    dx_low,
-    dy_high,
-    dy_low,
-    planes_out,
-    dz,
-    forward_x,
-    backward_x,
-    forward_y,
-    backward_y,
-    gain,
-    code_mask,
-    code_spread,
-    warped_ref,
-    gradient_ref,
-    code_send,
-    code_recv,
-    image_send,
-    image_recv,
-    halo_send,
-    halo_recv,
-    back_send,
-    back_recv,
-    code_sems,
-    image_sems,
-    halo_sems,
-    back_sems,
-):
+def body(n, names, template_hbm, image_hbm, owner_hbm, offset_hbm, level_hbm, *refs):
+    tables_hbm = refs[: len(names)]
+    (out_ref,) = refs[len(names) : len(names) + 1]
+    refs = refs[len(names) + 1 :]
+    template_ref, image_ref, owner_ref, offset_ref, level_ref = refs[:5]
+    table = dict(zip(names, refs[5 : 5 + len(names)]))
+    (
+        code_send,
+        code_recv,
+        image_send,
+        image_recv,
+        halo_send,
+        halo_recv,
+        back_send,
+        back_recv,
+        load_sems,
+        code_sems,
+        image_sems,
+        halo_sems,
+        back_sems,
+    ) = refs[5 + len(names) :]
+    sources = (template_hbm, image_hbm, owner_hbm, offset_hbm, level_hbm) + tables_hbm
+    targets = refs[: 5 + len(names)]
+    loads = {
+        key: pltpu.make_async_copy(source, target, load_sems.at[at])
+        for at, (key, source, target) in enumerate(
+            zip(("template", "image", "owner", "offset", "level") + names, sources, targets)
+        )
+    }
+    order = ("template", "early", "owner", "offset", "level", "spread", "image")
+    for key in order + tuple(key for key in names if key not in order):
+        loads[key].start()
+
+    def loaded(*keys):
+        for key in keys:
+            loads[key].wait()
+
     me = lax.axis_index("pencil")
     rows, planes, ny = template_ref.shape
     m = n * rows * ZB
@@ -383,19 +381,32 @@
 
         lax.fori_loop(1, n, step, 0)
 
+    def sort_image(slot, ref):
+        value = ref[...].reshape(m, ny)
+        stacked = jnp.concatenate([value[:, :half], value[:, half:]], axis=0)
+        message = dot(table["early"][: 2 * m], stacked).astype(jnp.bfloat16)
+        image_send[slot] = message.reshape(n, 2 * ZB * rows, half)
+
+    loaded("template", "early")
+    sort_image(0, template_ref)
+    loaded("owner", "offset", "level", "spread")
+    shift = (planes // ZB * per).bit_length() - 1
+    base = owner_ref[...] * rows + lax.shift_right_logical(
+        offset_ref[...], jnp.full(offset_ref.shape, shift, jnp.int32)
+    )
+    base = base.astype(jnp.float32)
+    level = level_ref[...].astype(jnp.float32)
+    mask = table["early"][2 * m :].astype(jnp.float32)
     codes = jnp.zeros((m, 128), jnp.float32)
-    for j in range(4):
-        codes += dot(code_mask[...] * code_ref[j : j + 1, :], code_spread[j])
+    for j, line in enumerate((base[0:1], base[1:2], level[0:1], level[1:2])):
+        codes += dot((mask * line).astype(jnp.bfloat16), table["spread"][j])
     code_send[...] = codes.reshape(n, ZB * rows, 128)
-    both = jnp.concatenate(
-        [template_ref[...].reshape(m, ny), image_ref[...].reshape(m, ny)], axis=0
-    )
-    image_send[...] = (
-        dot(to_message[...], both).astype(jnp.bfloat16).reshape(n, 2 * ZB * rows, ny)
-    )
     pl.semaphore_wait(barrier, n - 1)
     scatter(code_send, code_recv, code_sems)
-    scatter(image_send, image_recv, image_sems)
+    scatter(image_send.at[0], image_recv.at[0], image_sems.at[0])
+    loaded("image")
+    sort_image(1, image_ref)
+    scatter(image_send.at[1], image_recv.at[1], image_sems.at[1])
 
     collect(code_send, code_recv, code_sems)
     code = code_recv[...].reshape(m, 128)
@@ -419,19 +430,23 @@
         low = (taps - high.astype(jnp.float32)).astype(jnp.bfloat16)
         return high, low
 
-    first = [stencil(0, g, first_x[...]) for g in range(per)]
-    collect(image_send, image_recv, image_sems)
-    images = image_recv[...].reshape(2 * m, ny)
+    loaded("first", "second")
+    first = [stencil(0, g, table["first"][g * SEG // half]) for g in range(per)]
+    second = [stencil(1, g, table["second"][...]) for g in range(per)]
+    collect(image_send.at[0], image_recv.at[0], image_sems.at[0])
+    template = image_recv[0].reshape(2 * m, half)
     warped = []
     for g in range(per):
+        at = g * SEG % half
+        seg = template[:, at : at + SEG]
         high, low = first[g]
-        seg = images[:, g * SEG : (g + 1) * SEG]
         seg = (dot(high, seg) + dot(low, seg)).astype(jnp.bfloat16)
-        high, low = stencil(1, g, second_x[...])
+        high, low = second[g]
         warped.append((dot(high, seg) + dot(low, seg)).astype(jnp.bfloat16))
     warped = jnp.concatenate(warped, axis=1)
 
-    halo_send[...] = dot(planes_out[...], warped).astype(jnp.bfloat16).reshape(2, nx, ny)
+    loaded("ends", "lines")
+    halo_send[...] = dot(table["ends"][...], warped).astype(jnp.bfloat16).reshape(2, nx, ny)
     halos = [
         pltpu.make_async_remote_copy(
             src_ref=halo_send.at[side],
@@ -448,39 +463,41 @@
 
     def send_back(slot, value):
         stacked = jnp.concatenate([value[:, :half], value[:, half:]], axis=0)
-        message = dot(line_message[...], stacked).astype(jnp.bfloat16)
+        message = dot(table["lines"][: 2 * m], stacked).astype(jnp.bfloat16)
         back_send[slot] = message.reshape(n, 2 * ZB * rows, half)
         scatter(back_send.at[slot], back_recv.at[slot], back_sems.at[slot])
 
     send_back(0, warped)
-    residual = dot(line_second[...], images) - warped.astype(jnp.float32)
+    loaded("dx", "dy", "x", "fy", "by", "gain")
+    slope_x = dot(table["dx"][:m], warped) + dot(table["dx"][m:], warped)
+    collect(image_send.at[1], image_recv.at[1], image_sems.at[1])
+    image = dot(table["lines"][2 * m : 4 * m], image_recv[1].reshape(2 * m, half))
+    image = jnp.concatenate([image[:m], image[m:]], axis=1)
+    residual = image - warped.astype(jnp.float32)
 
     def smooth(slot, slope):
         force = (slope * residual).astype(jnp.bfloat16)
-        spectrum = dot(force, forward_y[...]).astype(jnp.bfloat16)
-        spectrum = (dot(forward_x[...], spectrum) * gain[...]).astype(jnp.bfloat16)
-        spectrum = dot(backward_x[...], spectrum).astype(jnp.bfloat16)
-        send_back(slot, dot(spectrum, backward_y[...]).astype(jnp.bfloat16))
-
-    smooth(1, dot(dx_high[...], warped) + dot(dx_low[...], warped))
-    smooth(2, dot(warped, dy_high[...]) + dot(warped, dy_low[...]))
+        spectrum = dot(force, table["fy"][...]).astype(jnp.bfloat16)
+        spectrum = dot(table["x"][:m], spectrum) * table["gain"][...]
+        spectrum = dot(table["x"][m:], spectrum.astype(jnp.bfloat16)).astype(jnp.bfloat16)
+        send_back(slot, dot(spectrum, table["by"][...]).astype(jnp.bfloat16))
+
+    smooth(1, slope_x)
+    smooth(2, dot(warped, table["dy"][:ny]) + dot(warped, table["dy"][ny:]))
     for halo in halos:
         halo.wait_recv()
-    smooth(
-        3, dot(dz[...], jnp.concatenate([warped, halo_recv[0], halo_recv[1]], axis=0))
-    )
+    near = jnp.concatenate([warped, halo_recv[0], halo_recv[1]], axis=0)
+    smooth(3, dot(table["lines"][6 * m :], near))
 
     for slot in range(4):
         collect(back_send.at[slot], back_recv.at[slot], back_sems.at[slot])
-        home = dot(from_message[...], back_recv[slot].reshape(2 * m, half))
-        home = jnp.concatenate([home[:m], home[m:]], axis=1).reshape(rows, planes, ny)
-        if slot == 0:
-            warped_ref[...] = home.astype(jnp.bfloat16)
-        else:
-            gradient_ref[slot - 1] = velocity_ref[slot - 1] + home
+        home = dot(table["lines"][4 * m : 6 * m], back_recv[slot].reshape(2 * m, half))
+        home = jnp.concatenate([home[:m], home[m:]], axis=1).astype(jnp.bfloat16)
+        out_ref[slot] = home.reshape(rows, planes, ny)
 
     drain(code_send, code_recv, code_sems)
-    drain(image_send, image_recv, image_sems)
+    for slot in range(2):
+        drain(image_send.at[slot], image_recv.at[slot], image_sems.at[slot])
     for halo in halos:
         halo.wait_send()
     for slot in range(4):
@@ -490,48 +507,50 @@
 def by_groups(template, reference_image, velocity, dep_owner, dep_offset, dep_weight):
     n = lax.axis_size("pencil")
     rows, planes, ny = template.shape
-    per_row = planes // ZB * (ny // SEG)
     m = n * rows * ZB
-    base = (dep_owner * rows + dep_offset // per_row) % (n * rows)
-    codes = jnp.concatenate([base, dep_weight], axis=0).astype(jnp.bfloat16)
-    constants = [jnp.asarray(t) for t in tables(n, rows, planes, ny)]
-    vmem = pl.BlockSpec(memory_space=pltpu.VMEM)
+    held = tables(n, rows, planes, ny)
+    names = tuple(held)
+    constants = [jnp.asarray(held[name]) for name in names]
+    operands = (template, reference_image, dep_owner, dep_offset, dep_weight, *constants)
     b16, f32 = jnp.bfloat16, jnp.float32
-    return pl.pallas_call(
-        functools.partial(body, n),
-        out_shape=(
-            jax.ShapeDtypeStruct(template.shape, b16),
-            jax.ShapeDtypeStruct(velocity.shape, f32),
-        ),
-        in_specs=[vmem] * (4 + len(constants)),
-        out_specs=(vmem, vmem),
-        scratch_shapes=[
+    message = (n, 2 * ZB * rows, ny // 2)
+    out = pl.pallas_call(
+        functools.partial(body, n, names),
+        out_shape=jax.ShapeDtypeStruct((4,) + template.shape, b16),
+        in_specs=[pl.BlockSpec(memory_space=pltpu.HBM)] * len(operands),
+        out_specs=pl.BlockSpec(memory_space=pltpu.VMEM),
+        scratch_shapes=[pltpu.VMEM(array.shape, array.dtype) for array in operands]
+        + [
             pltpu.VMEM((n, ZB * rows, 128), f32),
             pltpu.VMEM((n, ZB * rows, 128), f32),
-            pltpu.VMEM((n, 2 * ZB * rows, ny), b16),
-            pltpu.VMEM((n, 2 * ZB * rows, ny), b16),
+            pltpu.VMEM((2,) + message, b16),
+            pltpu.VMEM((2,) + message, b16),
             pltpu.VMEM((2, n * rows, ny), b16),
             pltpu.VMEM((2, n * rows, ny), b16),
-            pltpu.VMEM((4, n, 2 * ZB * rows, ny // 2), b16),
-            pltpu.VMEM((4, n, 2 * ZB * rows, ny // 2), b16),
+            pltpu.VMEM((4,) + message, b16),
+            pltpu.VMEM((4,) + message, b16),
+            pltpu.SemaphoreType.DMA((len(operands),)),
             pltpu.SemaphoreType.DMA((2, n)),
-            pltpu.SemaphoreType.DMA((2, n)),
+            pltpu.SemaphoreType.DMA((2, 2, n)),
             pltpu.SemaphoreType.DMA((2, 2)),
             pltpu.SemaphoreType.DMA((4, 2, n)),
         ],
         compiler_params=pltpu.CompilerParams(
-            collective_id=0, has_side_effects=True, vmem_limit_bytes=40 * 1024 * 1024
+            collective_id=0, has_side_effects=True, vmem_limit_bytes=60 * 1024 * 1024
         ),
         cost_estimate=pl.CostEstimate(
             flops=24 * m * ny * ny, bytes_accessed=8 * m * ny * 4, transcendentals=0
         ),
-    )(template, reference_image, velocity, codes, *constants)
+    )(*operands)
+    return out[0], velocity + out[1:].astype(f32)
 
 
 def local(template, *others):
     n = lax.axis_size("pencil")
-    rows, planes, _ = template.shape
-    if n > 2 and planes == n * ZB and rows * ZB == 8 and n * rows <= 256:
+    rows, planes, ny = template.shape
+    per_row = planes // ZB * (ny // SEG)
+    whole = planes == n * ZB and ny % (2 * SEG) == 0 and per_row & (per_row - 1) == 0
+    if n > 2 and whole and rows * ZB == 8 and n * rows <= 256:
         return by_groups(template, *others)
     return general(template, *others)
 

time: 55.7 us -> 36.4 us (0.65); the launches traced: 54.6 us -> 36.2 us
  local copies, waits for them, and re-layouts: 20.5 us -> 1.57 us
  other arithmetic: 1.42 us -> 1.99 us
    unnamed x46 -> x2, local copies, waits for them, and re-layouts: 20.5 us -> 0.01 us
    add x0 -> x1, other arithmetic: none -> 1.99 us  [by_groups(): return (out[0], velocity + out[1:].astype(f32))]
    squeeze x0 -> x1, local copies, waits for them, and re-layouts: none -> 1.57 us  [by_groups(): return (out[0], velocity + out[1:].astype(f32))]
    another operation x2 -> x0, other arithmetic: 1.41 us -> none
where the time goes in v2:
time: 36.4 us; the launch traced here: 36.2 us
  Pallas kernels  32 us (88%)
  other arithmetic  1.99 us (5%)
  local copies, waits for them, and re-layouts  1.57 us (4%)
  between operations  0.65 us (2%)
    pallas_call x1, Pallas kernels, by_groups(): pl.pallas_call(functools.partial(body, n, names), out_shape=jax.ShapeDtyp...  32 us
    add x1, other arithmetic, by_groups(): return (out[0], velocity + out[1:].astype(f32))  1.99 us
    squeeze x1, local copies, waits for them, and re-layouts, by_groups(): return (out[0], velocity + out[1:].astype(f32))  1.57 us

profile of v2, /device:TPU:0, one launch (start us, length us, event | category | flops | bytes accessed | tf_op | source)
XLA Modules:
  0.0 36.2 jit_solution(15042874261852179330)
XLA Ops:
  0.6 0.0 copy-start
  0.6 32.0 %shard_map.185 = bf16[4,4,32,512]{3,2,1,0:T(8,128)(2,1)} custom-call(bf16[4,32,512]{2,1,0:T(8,128)(2,1)} %template_hbm.1, bf16[4,32,512]{2,1,0:T(8,128)(2,1)} %image_hbm.1, s32[2,256]{1,0:T(2,128)} %owner_hbm.1, s32[2,256]{1,0:T(2,128)} %offset_hbm.1, s32[2,256]{1,0:T(2,128)} %level_hbm.1, bf16[384,256]{1,0:T(8,128)(2,1)} %constant.24.clone.refs_0_, ...), custom_call_target="tpu_custom_call" | custom-call | flops 805306368 | bytes 2097152 | tf_op jit(solution)/shard_map/pallas_call | solution.py:517
  32.7 1.6 %slice_bitcast_fusion = bf16[4,32,512]{2,1,0:T(8,128)(2,1)} fusion(bf16[4,4,32,512]{3,2,1,0:T(8,128)(2,1)} %shard_map.185), kind=kLoop, calls=%fused_computation.1 | loop fusion | bytes 262144 | tf_op jit(solution)/shard_map/squeeze | solution.py:545
  34.2 0.0 copy-done
  34.2 2.0 %convert_add_fusion = f32[3,4,32,512]{3,2,1,0:T(8,128)} fusion(f32[3,4,32,512]{3,2,1,0:T(8,128)S(1)} %copy-done, bf16[4,4,32,512]{3,2,1,0:T(8,128)(2,1)} %shard_map.185), kind=kLoop, calls=%fused_computation | loop fusion | flops 393216 | bytes 1966080 | tf_op jit(solution)/shard_map/add | solution.py:545
Async XLA Ops:
  0.6 33.6 %copy-start = (f32[3,4,32,512]{3,2,1,0:T(8,128)S(1)}, f32[3,4,32,512]{3,2,1,0:T(8,128)}, u32[]{:S(2)}) copy-start(f32[3,4,32,512]{3,2,1,0:T(8,128)} %param.20) | copy-start | bytes 2359300

commit v3 on v2

--- a/solution.py
+++ b/solution.py
@@ -275,15 +275,15 @@
         "spread": b16(code_spread),
         "first": f32(first_x),
         "second": f32(second_x),
-        "lines": b16(np.concatenate([line_message, line_message.T, to_message.T, dz])),
+        "lines": b16(np.concatenate([line_message, line_message.T, dz])),
         "ends": b16(np.concatenate([plane_last, plane_first])),
-        "dx": np.concatenate([*split_pair(dx)]),
-        "dy": np.concatenate([*split_pair(dy)]),
+        "dx": np.concatenate(split_pair(dx)),
+        "dy": np.concatenate(split_pair(dy)),
         "x": b16(np.concatenate([forward, backward])),
         "fy": b16(fy),
         "by": b16(by),
         "gain": f32(gain),
-    }
+    }, b16(to_message.T)
 
 
 def dot(a, b):
@@ -292,7 +292,7 @@
 
 def body(n, names, template_hbm, image_hbm, owner_hbm, offset_hbm, level_hbm, *refs):
     tables_hbm = refs[: len(names)]
-    (out_ref,) = refs[len(names) : len(names) + 1]
+    (back_recv,) = refs[len(names) : len(names) + 1]
     refs = refs[len(names) + 1 :]
     template_ref, image_ref, owner_ref, offset_ref, level_ref = refs[:5]
     table = dict(zip(names, refs[5 : 5 + len(names)]))
@@ -304,12 +304,12 @@
         halo_send,
         halo_recv,
         back_send,
-        back_recv,
         load_sems,
         code_sems,
         image_sems,
         halo_sems,
         back_sems,
+        own_sems,
     ) = refs[5 + len(names) :]
     sources = (template_hbm, image_hbm, owner_hbm, offset_hbm, level_hbm) + tables_hbm
     targets = refs[: 5 + len(names)]
@@ -349,37 +349,36 @@
 
     lax.fori_loop(1, n, greet, 0)
 
-    def copy(send, recv, sems, off, slot):
-        return pltpu.make_async_remote_copy(
-            src_ref=send.at[lax.rem(me + off, n)],
-            dst_ref=recv.at[slot],
-            send_sem=sems.at[0, off],
-            recv_sem=sems.at[1, off],
-            device_id={"pencil": lax.rem(me + off, n)},
-            device_id_type=pl.DeviceIdType.MESH,
-        )
-
     def scatter(send, recv, sems):
         def step(off, carry):
-            copy(send, recv, sems, off, me).start()
+            to = lax.rem(me + off, n)
+            pltpu.make_async_remote_copy(
+                src_ref=send.at[to],
+                dst_ref=recv.at[me],
+                send_sem=sems.at[0],
+                recv_sem=sems.at[1],
+                device_id={"pencil": to},
+                device_id_type=pl.DeviceIdType.MESH,
+            ).start()
             return carry
 
         lax.fori_loop(1, n, step, 0)
-        recv[me] = send[me]
+
+    def everything(send, recv, sems):
+        return pltpu.make_async_remote_copy(
+            src_ref=send.at[pl.ds(0, n - 1)],
+            dst_ref=recv.at[pl.ds(0, n - 1)],
+            send_sem=sems.at[0],
+            recv_sem=sems.at[1],
+            device_id={"pencil": after},
+            device_id_type=pl.DeviceIdType.MESH,
+        )
 
     def collect(send, recv, sems):
-        def step(off, carry):
-            copy(send, recv, sems, off, lax.rem(me + n - off, n)).wait_recv()
-            return carry
-
-        lax.fori_loop(1, n, step, 0)
+        everything(send, recv, sems).wait_recv()
 
     def drain(send, recv, sems):
-        def step(off, carry):
-            copy(send, recv, sems, off, me).wait_send()
-            return carry
-
-        lax.fori_loop(1, n, step, 0)
+        everything(send, recv, sems).wait_send()
 
     def sort_image(slot, ref):
         value = ref[...].reshape(m, ny)
@@ -404,9 +403,12 @@
     pl.semaphore_wait(barrier, n - 1)
     scatter(code_send, code_recv, code_sems)
     scatter(image_send.at[0], image_recv.at[0], image_sems.at[0])
+    code_recv[me] = code_send[me]
+    image_recv[0, me] = image_send[0, me]
     loaded("image")
     sort_image(1, image_ref)
     scatter(image_send.at[1], image_recv.at[1], image_sems.at[1])
+    image_recv[1, me] = image_send[1, me]
 
     collect(code_send, code_recv, code_sems)
     code = code_recv[...].reshape(m, 128)
@@ -461,11 +463,17 @@
     for halo in halos:
         halo.start()
 
+    def own(slot):
+        return pltpu.make_async_copy(
+            back_send.at[slot, me], back_recv.at[slot, me], own_sems.at[slot]
+        )
+
     def send_back(slot, value):
         stacked = jnp.concatenate([value[:, :half], value[:, half:]], axis=0)
         message = dot(table["lines"][: 2 * m], stacked).astype(jnp.bfloat16)
         back_send[slot] = message.reshape(n, 2 * ZB * rows, half)
         scatter(back_send.at[slot], back_recv.at[slot], back_sems.at[slot])
+        own(slot).start()
 
     send_back(0, warped)
     loaded("dx", "dy", "x", "fy", "by", "gain")
@@ -487,13 +495,7 @@
     for halo in halos:
         halo.wait_recv()
     near = jnp.concatenate([warped, halo_recv[0], halo_recv[1]], axis=0)
-    smooth(3, dot(table["lines"][6 * m :], near))
-
-    for slot in range(4):
-        collect(back_send.at[slot], back_recv.at[slot], back_sems.at[slot])
-        home = dot(table["lines"][4 * m : 6 * m], back_recv[slot].reshape(2 * m, half))
-        home = jnp.concatenate([home[:m], home[m:]], axis=1).astype(jnp.bfloat16)
-        out_ref[slot] = home.reshape(rows, planes, ny)
+    smooth(3, dot(table["lines"][4 * m :], near))
 
     drain(code_send, code_recv, code_sems)
     for slot in range(2):
@@ -501,24 +503,65 @@
     for halo in halos:
         halo.wait_send()
     for slot in range(4):
+        own(slot).wait()
+        collect(back_send.at[slot], back_recv.at[slot], back_sems.at[slot])
         drain(back_send.at[slot], back_recv.at[slot], back_sems.at[slot])
+
+
+def finish(
+    back_hbm,
+    velocity_ref,
+    sort_ref,
+    warped_hbm,
+    gradient_hbm,
+    back_ref,
+    warped_ref,
+    gradient_ref,
+    load_sems,
+    store_sems,
+):
+    rows, planes, ny = warped_ref.shape
+    m = rows * planes
+    loads = [
+        pltpu.make_async_copy(back_hbm.at[slot], back_ref.at[slot], load_sems.at[slot])
+        for slot in range(4)
+    ]
+    stores = [pltpu.make_async_copy(warped_ref, warped_hbm, store_sems.at[0])] + [
+        pltpu.make_async_copy(gradient_ref.at[c], gradient_hbm.at[c], store_sems.at[1 + c])
+        for c in range(3)
+    ]
+    for load in loads:
+        load.start()
+    for slot in range(4):
+        loads[slot].wait()
+        home = dot(sort_ref[...], back_ref[slot].reshape(2 * m, ny // 2))
+        home = jnp.concatenate([home[:m], home[m:]], axis=1).reshape(rows, planes, ny)
+        if slot == 0:
+            warped_ref[...] = home.astype(jnp.bfloat16)
+        else:
+            gradient_ref[slot - 1] = velocity_ref[slot - 1] + home
+        stores[slot].start()
+    for store in stores:
+        store.wait()
 
 
 def by_groups(template, reference_image, velocity, dep_owner, dep_offset, dep_weight):
     n = lax.axis_size("pencil")
     rows, planes, ny = template.shape
     m = n * rows * ZB
-    held = tables(n, rows, planes, ny)
+    held, sort_rows = tables(n, rows, planes, ny)
     names = tuple(held)
     constants = [jnp.asarray(held[name]) for name in names]
     operands = (template, reference_image, dep_owner, dep_offset, dep_weight, *constants)
     b16, f32 = jnp.bfloat16, jnp.float32
     message = (n, 2 * ZB * rows, ny // 2)
-    out = pl.pallas_call(
+    hbm = pl.BlockSpec(memory_space=pltpu.HBM)
+    vmem = pl.BlockSpec(memory_space=pltpu.VMEM)
+    back = pl.pallas_call(
         functools.partial(body, n, names),
-        out_shape=jax.ShapeDtypeStruct((4,) + template.shape, b16),
-        in_specs=[pl.BlockSpec(memory_space=pltpu.HBM)] * len(operands),
-        out_specs=pl.BlockSpec(memory_space=pltpu.VMEM),
+        out_shape=jax.ShapeDtypeStruct((4,) + message, b16),
+        in_specs=[hbm] * len(operands),
+        out_specs=hbm,
         scratch_shapes=[pltpu.VMEM(array.shape, array.dtype) for array in operands]
         + [
             pltpu.VMEM((n, ZB * rows, 128), f32),
@@ -528,12 +571,12 @@
             pltpu.VMEM((2, n * rows, ny), b16),
             pltpu.VMEM((2, n * rows, ny), b16),
             pltpu.VMEM((4,) + message, b16),
-            pltpu.VMEM((4,) + message, b16),
             pltpu.SemaphoreType.DMA((len(operands),)),
-            pltpu.SemaphoreType.DMA((2, n)),
-            pltpu.SemaphoreType.DMA((2, 2, n)),
+            pltpu.SemaphoreType.DMA((2,)),
             pltpu.SemaphoreType.DMA((2, 2)),
-            pltpu.SemaphoreType.DMA((4, 2, n)),
+            pltpu.SemaphoreType.DMA((2, 2)),
+            pltpu.SemaphoreType.DMA((4, 2)),
+            pltpu.SemaphoreType.DMA((4,)),
         ],
         compiler_params=pltpu.CompilerParams(
             collective_id=0, has_side_effects=True, vmem_limit_bytes=60 * 1024 * 1024
@@ -542,7 +585,26 @@
             flops=24 * m * ny * ny, bytes_accessed=8 * m * ny * 4, transcendentals=0
         ),
     )(*operands)
-    return out[0], velocity + out[1:].astype(f32)
+    return pl.pallas_call(
+        finish,
+        out_shape=(
+            jax.ShapeDtypeStruct(template.shape, b16),
+            jax.ShapeDtypeStruct(velocity.shape, f32),
+        ),
+        in_specs=[hbm, vmem, vmem],
+        out_specs=(hbm, hbm),
+        scratch_shapes=[
+            pltpu.VMEM(back.shape, b16),
+            pltpu.VMEM(template.shape, b16),
+            pltpu.VMEM(velocity.shape, f32),
+            pltpu.SemaphoreType.DMA((4,)),
+            pltpu.SemaphoreType.DMA((4,)),
+        ],
+        compiler_params=pltpu.CompilerParams(vmem_limit_bytes=60 * 1024 * 1024),
+        cost_estimate=pl.CostEstimate(
+            flops=16 * m * m * ny, bytes_accessed=4 * m * ny * 8, transcendentals=0
+        ),
+    )(back, velocity, jnp.asarray(sort_rows))
 
 
 def local(template, *others):

time: 36.4 us -> 33 us (0.907)
  other arithmetic: 1.99 us -> 0 us
  local copies, waits for them, and re-layouts: 1.57 us -> 0 us
    pallas_call x0 -> x1, Pallas kernels: none -> 3.69 us  [by_groups(): pl.pallas_call(finish, out_shape=(jax.ShapeDtypeStruct(template.shape, b1...]
    pallas_call x1, Pallas kernels: 32 us -> 28.6 us  [by_groups(): pl.pallas_call(functools.partial(body, n, names), out_shape=jax.ShapeDtyp...]
    add x1 -> x0, other arithmetic: 1.99 us -> none  [by_groups(): return (out[0], velocity + out[1:].astype(f32))]
    squeeze x1 -> x0, local copies, waits for them, and re-layouts: 1.57 us -> none  [by_groups(): return (out[0], velocity + out[1:].astype(f32))]
where the time goes in v3:
time: 33 us; the launch traced here: 32.9 us
  Pallas kernels  32.2 us (98%)
  between operations  0.64 us (2%)
    pallas_call x1, Pallas kernels, by_groups(): pl.pallas_call(functools.partial(body, n, names), out_shape=jax.ShapeDtyp...  28.6 us
    pallas_call x1, Pallas kernels, by_groups(): pl.pallas_call(finish, out_shape=(jax.ShapeDtypeStruct(template.shape, b1...  3.69 us

profile of v3, /device:TPU:0, one launch (start us, length us, event | category | flops | bytes accessed | tf_op | source)
XLA Modules:
  0.0 32.9 jit_solution(14577902329271255743)
XLA Ops:
  0.6 28.6 %shard_map.194.back_hbm = bf16[4,16,16,256]{3,2,1,0:T(8,128)(2,1)} custom-call(bf16[4,32,512]{2,1,0:T(8,128)(2,1)} %template_hbm.1, bf16[4,32,512]{2,1,0:T(8,128)(2,1)} %image_hbm.1, s32[2,256]{1,0:T(2,128)} %owner_hbm.1, s32[2,256]{1,0:T(2,128)} %offset_hbm.1, s32[2,256]{1,0:T(2,128)} %level_hbm.1, bf16[384,256]{1,0:T(8,128)(2,1)} %constant.26.clone.refs_0_, ...), custom_call_target="tpu_custom_call" | custom-call | flops 805306368 | bytes 2097152 | tf_op jit(solution)/shard_map/pallas_call | solution.py:560
  29.2 3.7 %shard_map.195 = (bf16[4,32,512]{2,1,0:T(8,128)(2,1)}, f32[3,4,32,512]{3,2,1,0:T(8,128)}) custom-call(bf16[4,16,16,256]{3,2,1,0:T(8,128)(2,1)} %shard_map.194.back_hbm, f32[3,4,32,512]{3,2,1,0:T(8,128)} %velocity_ref.1, bf16[256,256]{1,0:T(8,128)(2,1)} %constant.38.clone.sort_ref), custom_call_target="tpu_custom_call" | custom-call | flops 134217728 | bytes 2097152 | tf_op jit(solution)/shard_map/pallas_call | solution.py:588

commit v4 on v3

--- a/solution.py
+++ b/solution.py
@@ -337,21 +337,16 @@
     before = lax.rem(me + n - 1, n)
 
     barrier = pltpu.get_barrier_semaphore()
-
-    def greet(off, carry):
+    partners = [
+        lax.rem(me + off, n) for off in sorted(range(1, n), key=lambda off: abs(off - n // 2))
+    ]
+    for to in partners:
         pl.semaphore_signal(
-            barrier,
-            inc=1,
-            device_id={"pencil": lax.rem(me + off, n)},
-            device_id_type=pl.DeviceIdType.MESH,
-        )
-        return carry
-
-    lax.fori_loop(1, n, greet, 0)
+            barrier, inc=1, device_id={"pencil": to}, device_id_type=pl.DeviceIdType.MESH
+        )
 
     def scatter(send, recv, sems):
-        def step(off, carry):
-            to = lax.rem(me + off, n)
+        for to in partners:
             pltpu.make_async_remote_copy(
                 src_ref=send.at[to],
                 dst_ref=recv.at[me],
@@ -360,9 +355,6 @@
                 device_id={"pencil": to},
                 device_id_type=pl.DeviceIdType.MESH,
             ).start()
-            return carry
-
-        lax.fori_loop(1, n, step, 0)
 
     def everything(send, recv, sems):
         return pltpu.make_async_remote_copy(
@@ -510,11 +502,13 @@
 
 def finish(
     back_hbm,
-    velocity_ref,
-    sort_ref,
+    velocity_hbm,
+    sort_hbm,
     warped_hbm,
     gradient_hbm,
     back_ref,
+    velocity_ref,
+    sort_ref,
     warped_ref,
     gradient_ref,
     load_sems,
@@ -522,23 +516,33 @@
 ):
     rows, planes, ny = warped_ref.shape
     m = rows * planes
-    loads = [
-        pltpu.make_async_copy(back_hbm.at[slot], back_ref.at[slot], load_sems.at[slot])
+    sort = pltpu.make_async_copy(sort_hbm, sort_ref, load_sems.at[0])
+    backs = [
+        pltpu.make_async_copy(back_hbm.at[slot], back_ref.at[slot], load_sems.at[1 + slot])
         for slot in range(4)
+    ]
+    velocities = [
+        pltpu.make_async_copy(velocity_hbm.at[c], velocity_ref.at[c], load_sems.at[5 + c])
+        for c in range(3)
     ]
     stores = [pltpu.make_async_copy(warped_ref, warped_hbm, store_sems.at[0])] + [
         pltpu.make_async_copy(gradient_ref.at[c], gradient_hbm.at[c], store_sems.at[1 + c])
         for c in range(3)
     ]
-    for load in loads:
-        load.start()
-    for slot in range(4):
-        loads[slot].wait()
+    sort.start()
+    for slot in (1, 2, 3, 0):
+        backs[slot].start()
+        if slot > 0:
+            velocities[slot - 1].start()
+    sort.wait()
+    for slot in (1, 2, 3, 0):
+        backs[slot].wait()
         home = dot(sort_ref[...], back_ref[slot].reshape(2 * m, ny // 2))
         home = jnp.concatenate([home[:m], home[m:]], axis=1).reshape(rows, planes, ny)
         if slot == 0:
             warped_ref[...] = home.astype(jnp.bfloat16)
         else:
+            velocities[slot - 1].wait()
             gradient_ref[slot - 1] = velocity_ref[slot - 1] + home
         stores[slot].start()
     for store in stores:
@@ -556,7 +560,6 @@
     b16, f32 = jnp.bfloat16, jnp.float32
     message = (n, 2 * ZB * rows, ny // 2)
     hbm = pl.BlockSpec(memory_space=pltpu.HBM)
-    vmem = pl.BlockSpec(memory_space=pltpu.VMEM)
     back = pl.pallas_call(
         functools.partial(body, n, names),
         out_shape=jax.ShapeDtypeStruct((4,) + message, b16),
@@ -591,13 +594,15 @@
             jax.ShapeDtypeStruct(template.shape, b16),
             jax.ShapeDtypeStruct(velocity.shape, f32),
         ),
-        in_specs=[hbm, vmem, vmem],
+        in_specs=[hbm, hbm, hbm],
         out_specs=(hbm, hbm),
         scratch_shapes=[
             pltpu.VMEM(back.shape, b16),
+            pltpu.VMEM(velocity.shape, f32),
+            pltpu.VMEM(sort_rows.shape, b16),
             pltpu.VMEM(template.shape, b16),
             pltpu.VMEM(velocity.shape, f32),
-            pltpu.SemaphoreType.DMA((4,)),
+            pltpu.SemaphoreType.DMA((8,)),
             pltpu.SemaphoreType.DMA((4,)),
         ],
         compiler_params=pltpu.CompilerParams(vmem_limit_bytes=60 * 1024 * 1024),

time: 33 us -> 32.6 us (0.988)
  Pallas kernels: 32.2 us -> 31.8 us
    pallas_call x1, Pallas kernels: 3.69 us -> 2.67 us  [by_groups(): pl.pallas_call(finish, out_shape=(jax.ShapeDtypeStruct(template.shape, b1...]
    pallas_call x1, Pallas kernels: 28.6 us -> 29.1 us  [by_groups(): pl.pallas_call(functools.partial(body, n, names), out_shape=jax.ShapeDtyp...]
where the time goes in v4:
time: 32.6 us; the launch traced here: 32.4 us
  Pallas kernels  31.8 us (98%)
  between operations  0.64 us (2%)
    pallas_call x1, Pallas kernels, by_groups(): pl.pallas_call(functools.partial(body, n, names), out_shape=jax.ShapeDtyp...  29.1 us
    pallas_call x1, Pallas kernels, by_groups(): pl.pallas_call(finish, out_shape=(jax.ShapeDtypeStruct(template.shape, b1...  2.67 us

profile of v4, /device:TPU:0, one launch (start us, length us, event | category | flops | bytes accessed | tf_op | source)
XLA Modules:
  0.0 32.4 jit_solution(16863146980951653286)
XLA Ops:
  0.6 29.1 %shard_map.194.back_hbm = bf16[4,16,16,256]{3,2,1,0:T(8,128)(2,1)} custom-call(bf16[4,32,512]{2,1,0:T(8,128)(2,1)} %template_hbm.1, bf16[4,32,512]{2,1,0:T(8,128)(2,1)} %image_hbm.1, s32[2,256]{1,0:T(2,128)} %owner_hbm.1, s32[2,256]{1,0:T(2,128)} %offset_hbm.1, s32[2,256]{1,0:T(2,128)} %level_hbm.1, bf16[384,256]{1,0:T(8,128)(2,1)} %constant.26.clone.refs_0_, ...), custom_call_target="tpu_custom_call" | custom-call | flops 805306368 | bytes 2097152 | tf_op jit(solution)/shard_map/pallas_call | solution.py:563
  29.8 2.7 %shard_map.195 = (bf16[4,32,512]{2,1,0:T(8,128)(2,1)}, f32[3,4,32,512]{3,2,1,0:T(8,128)}) custom-call(bf16[4,16,16,256]{3,2,1,0:T(8,128)(2,1)} %shard_map.194.back_hbm, f32[3,4,32,512]{3,2,1,0:T(8,128)} %velocity_hbm.1, bf16[256,256]{1,0:T(8,128)(2,1)} %constant.38.clone.sort_hbm), custom_call_target="tpu_custom_call" | custom-call | flops 134217728 | bytes 2097152 | tf_op jit(solution)/shard_map/pallas_call | solution.py:591

commit v5 on v4

--- a/solution.py
+++ b/solution.py
@@ -262,16 +262,21 @@
     lanes = np.arange(rows * groups * per)
     lane_row = lanes // (groups * per)
     lane_group = lanes // per % groups
-    code_mask = (lane_group[None, :] == (index // (ZB * rows))[:, None]) & (
-        lane_row[None, :] == (index % rows)[:, None]
-    )
+    code_mask = np.arange(n)[:, None] == lane_group[None, :]
     code_spread = np.zeros((4, lanes.size, 128))
     for j in range(4):
-        code_spread[j, lanes, j * per + lanes % per] = 1.0
+        code_spread[j, lanes, (lane_row * 4 + j) * per + lanes % per] = 1.0
+    code_lines = index[:, None] // (ZB * rows) == np.arange(n)[None, :]
+    out = np.arange(128)
+    code_rows = (out[None, :] // (4 * per)) == (index % rows)[:, None]
+    code_fold = (out[:, None] % (4 * per) == out[None, :]) & (out[:, None] < rows * 4 * per)
     b16 = lambda t: np.asarray(t, np.float64).astype(jnp.bfloat16)
     f32 = lambda t: np.asarray(t, np.float32)
     return {
-        "early": b16(np.concatenate([to_message, code_mask])),
+        "early": b16(to_message),
+        "mask": f32(code_mask),
+        "lay": b16(code_lines),
+        "fold": b16(np.concatenate([code_rows, code_fold])),
         "spread": b16(code_spread),
         "first": f32(first_x),
         "second": f32(second_x),
@@ -319,7 +324,7 @@
             zip(("template", "image", "owner", "offset", "level") + names, sources, targets)
         )
     }
-    order = ("template", "early", "owner", "offset", "level", "spread", "image")
+    order = ("template", "early", "owner", "offset", "level", "spread", "mask", "image", "lay", "fold")
     for key in order + tuple(key for key in names if key not in order):
         loads[key].start()
 
@@ -333,8 +338,14 @@
     nx = n * rows
     per = ny // SEG
     half = ny // 2
-    after = lax.rem(me + 1, n)
-    before = lax.rem(me + n - 1, n)
+    core = lax.axis_index("start")
+
+    def flip(at):
+        return at + lax.rem(core, 2) * (1 - 2 * lax.rem(at, 2))
+
+    group = flip(me)
+    after = flip(lax.rem(group + 1, n))
+    before = flip(lax.rem(group + n - 1, n))
 
     barrier = pltpu.get_barrier_semaphore()
     partners = [
@@ -345,11 +356,14 @@
             barrier, inc=1, device_id={"pencil": to}, device_id_type=pl.DeviceIdType.MESH
         )
 
-    def scatter(send, recv, sems):
-        for to in partners:
+    to_groups = [(to, flip(to), me) for to in partners]
+    to_homes = [(to, to, group) for to in partners]
+
+    def scatter(send, recv, sems, ways):
+        for to, part, place in ways:
             pltpu.make_async_remote_copy(
-                src_ref=send.at[to],
-                dst_ref=recv.at[me],
+                src_ref=send.at[part],
+                dst_ref=recv.at[place],
                 send_sem=sems.at[0],
                 recv_sem=sems.at[1],
                 device_id={"pencil": to},
@@ -375,35 +389,37 @@
     def sort_image(slot, ref):
         value = ref[...].reshape(m, ny)
         stacked = jnp.concatenate([value[:, :half], value[:, half:]], axis=0)
-        message = dot(table["early"][: 2 * m], stacked).astype(jnp.bfloat16)
+        message = dot(table["early"][...], stacked).astype(jnp.bfloat16)
         image_send[slot] = message.reshape(n, 2 * ZB * rows, half)
 
     loaded("template", "early")
     sort_image(0, template_ref)
-    loaded("owner", "offset", "level", "spread")
+    loaded("owner", "offset", "level", "spread", "mask")
     shift = (planes // ZB * per).bit_length() - 1
     base = owner_ref[...] * rows + lax.shift_right_logical(
         offset_ref[...], jnp.full(offset_ref.shape, shift, jnp.int32)
     )
     base = base.astype(jnp.float32)
     level = level_ref[...].astype(jnp.float32)
-    mask = table["early"][2 * m :].astype(jnp.float32)
-    codes = jnp.zeros((m, 128), jnp.float32)
+    codes = jnp.zeros((n, 128), jnp.float32)
     for j, line in enumerate((base[0:1], base[1:2], level[0:1], level[1:2])):
-        codes += dot((mask * line).astype(jnp.bfloat16), table["spread"][j])
-    code_send[...] = codes.reshape(n, ZB * rows, 128)
+        codes += dot((table["mask"][...] * line).astype(jnp.bfloat16), table["spread"][j])
+    code_send[...] = codes.reshape(n, 1, 128)
     pl.semaphore_wait(barrier, n - 1)
-    scatter(code_send, code_recv, code_sems)
-    scatter(image_send.at[0], image_recv.at[0], image_sems.at[0])
-    code_recv[me] = code_send[me]
-    image_recv[0, me] = image_send[0, me]
+    scatter(code_send, code_recv, code_sems, to_groups)
+    scatter(image_send.at[0], image_recv.at[0], image_sems.at[0], to_groups)
+    code_recv[me] = code_send[group]
+    image_recv[0, me] = image_send[0, group]
     loaded("image")
     sort_image(1, image_ref)
-    scatter(image_send.at[1], image_recv.at[1], image_sems.at[1])
-    image_recv[1, me] = image_send[1, me]
+    scatter(image_send.at[1], image_recv.at[1], image_sems.at[1], to_groups)
+    image_recv[1, me] = image_send[1, group]
 
     collect(code_send, code_recv, code_sems)
-    code = code_recv[...].reshape(m, 128)
+    loaded("lay", "fold")
+    code = dot(table["lay"][...], code_recv[...].reshape(n, 128).astype(jnp.bfloat16))
+    code = (code * table["fold"][:m].astype(jnp.float32)).astype(jnp.bfloat16)
+    code = dot(code, table["fold"][m:])
     t = (code + 0.5) / Q
     weights = (
         -t * (t - 1.0) * (t - 2.0) / 6.0,
@@ -457,14 +473,14 @@
 
     def own(slot):
         return pltpu.make_async_copy(
-            back_send.at[slot, me], back_recv.at[slot, me], own_sems.at[slot]
+            back_send.at[slot, me], back_recv.at[slot, group], own_sems.at[slot]
         )
 
     def send_back(slot, value):
         stacked = jnp.concatenate([value[:, :half], value[:, half:]], axis=0)
         message = dot(table["lines"][: 2 * m], stacked).astype(jnp.bfloat16)
         back_send[slot] = message.reshape(n, 2 * ZB * rows, half)
-        scatter(back_send.at[slot], back_recv.at[slot], back_sems.at[slot])
+        scatter(back_send.at[slot], back_recv.at[slot], back_sems.at[slot], to_homes)
         own(slot).start()
 
     send_back(0, warped)
@@ -567,8 +583,8 @@
         out_specs=hbm,
         scratch_shapes=[pltpu.VMEM(array.shape, array.dtype) for array in operands]
         + [
-            pltpu.VMEM((n, ZB * rows, 128), f32),
-            pltpu.VMEM((n, ZB * rows, 128), f32),
+            pltpu.VMEM((n, 1, 128), f32),
+            pltpu.VMEM((n, 1, 128), f32),
             pltpu.VMEM((2,) + message, b16),
             pltpu.VMEM((2,) + message, b16),
             pltpu.VMEM((2, n * rows, ny), b16),
@@ -617,7 +633,7 @@
     rows, planes, ny = template.shape
     per_row = planes // ZB * (ny // SEG)
     whole = planes == n * ZB and ny % (2 * SEG) == 0 and per_row & (per_row - 1) == 0
-    if n > 2 and whole and rows * ZB == 8 and n * rows <= 256:
+    if n > 2 and n % 2 == 0 and 4 * rows * (ny // SEG) <= 128 and whole and rows * ZB == 8 and n * rows <= 256:
         return by_groups(template, *others)
     return general(template, *others)
 

time: 32.6 us -> 31.4 us (0.963)
  Pallas kernels: 31.8 us -> 30.6 us
    pallas_call x1, Pallas kernels: 29.1 us -> 27.9 us  [by_groups(): pl.pallas_call(functools.partial(body, n, names), out_shape=jax.ShapeDtyp...]
where the time goes in v5:
time: 31.4 us; the launch traced here: 31.2 us
  Pallas kernels  30.6 us (97%)
  between operations  0.64 us (2%)
    pallas_call x1, Pallas kernels, by_groups(): pl.pallas_call(functools.partial(body, n, names), out_shape=jax.ShapeDtyp...  27.9 us
    pallas_call x1, Pallas kernels, by_groups(): pl.pallas_call(finish, out_shape=(jax.ShapeDtypeStruct(template.shape, b1...  2.66 us

profile of v5, /device:TPU:0, one launch (start us, length us, event | category | flops | bytes accessed | tf_op | source)
XLA Modules:
  0.0 31.2 jit_solution(5168616132485593809)
XLA Ops:
  0.6 27.9 %shard_map.221.back_hbm = bf16[4,16,16,256]{3,2,1,0:T(8,128)(2,1)} custom-call(bf16[4,32,512]{2,1,0:T(8,128)(2,1)} %template_hbm.1, bf16[4,32,512]{2,1,0:T(8,128)(2,1)} %image_hbm.1, s32[2,256]{1,0:T(2,128)} %owner_hbm.1, s32[2,256]{1,0:T(2,128)} %offset_hbm.1, s32[2,256]{1,0:T(2,128)} %level_hbm.1, bf16[256,256]{1,0:T(8,128)(2,1)} %constant.32.clone.refs_0_, ...), custom_call_target="tpu_custom_call" | custom-call | flops 805306368 | bytes 2097152 | tf_op jit(solution)/shard_map/pallas_call | solution.py:579
  28.6 2.7 %shard_map.222 = (bf16[4,32,512]{2,1,0:T(8,128)(2,1)}, f32[3,4,32,512]{3,2,1,0:T(8,128)}) custom-call(bf16[4,16,16,256]{3,2,1,0:T(8,128)(2,1)} %shard_map.221.back_hbm, f32[3,4,32,512]{3,2,1,0:T(8,128)} %velocity_hbm.1, bf16[256,256]{1,0:T(8,128)(2,1)} %constant.47.clone.sort_hbm), custom_call_target="tpu_custom_call" | custom-call | flops 134217728 | bytes 2097152 | tf_op jit(solution)/shard_map/pallas_call | solution.py:607

commit v6 on v5

--- a/solution.py
+++ b/solution.py
@@ -215,11 +215,9 @@
     wide_z = wide // rows % ZB
     wide_row = wide % rows
     slab = wide_half * m + wide_row * planes + wide_dev * ZB + wide_z
-    line = wide_half * m + wide_dev * (ZB * rows) + wide_z * rows + wide_row
     eye = np.eye(2 * m)
     to_message = eye[slab]
     from_message = eye[slab].T
-    line_message = eye[line]
     wide_x = wide_dev * rows + wide_row
     first_x = [
         np.where(
@@ -280,7 +278,7 @@
         "spread": b16(code_spread),
         "first": f32(first_x),
         "second": f32(second_x),
-        "lines": b16(np.concatenate([line_message, line_message.T, dz])),
+        "dz": b16(dz),
         "ends": b16(np.concatenate([plane_last, plane_first])),
         "dx": np.concatenate(split_pair(dx)),
         "dy": np.concatenate(split_pair(dy)),
@@ -338,6 +336,7 @@
     nx = n * rows
     per = ny // SEG
     half = ny // 2
+    each = ZB * rows
     core = lax.axis_index("start")
 
     def flip(at):
@@ -436,9 +435,7 @@
         taps = jnp.zeros_like(delta)
         for k in range(4):
             taps = jnp.where(delta == float(k), weights[k][:, at : at + 1], taps)
-        high = taps.astype(jnp.bfloat16)
-        low = (taps - high.astype(jnp.float32)).astype(jnp.bfloat16)
-        return high, low
+        return taps.astype(jnp.bfloat16)
 
     loaded("first", "second")
     first = [stencil(0, g, table["first"][g * SEG // half]) for g in range(per)]
@@ -449,13 +446,12 @@
     for g in range(per):
         at = g * SEG % half
         seg = template[:, at : at + SEG]
-        high, low = first[g]
-        seg = (dot(high, seg) + dot(low, seg)).astype(jnp.bfloat16)
-        high, low = second[g]
-        warped.append((dot(high, seg) + dot(low, seg)).astype(jnp.bfloat16))
+        seg = dot(first[g], seg).astype(jnp.bfloat16)
+        warped.append(dot(second[g], seg).astype(jnp.bfloat16))
     warped = jnp.concatenate(warped, axis=1)
-
-    loaded("ends", "lines")
+    warped_f = warped.astype(jnp.float32)
+
+    loaded("ends", "dz")
     halo_send[...] = dot(table["ends"][...], warped).astype(jnp.bfloat16).reshape(2, nx, ny)
     halos = [
         pltpu.make_async_remote_copy(
@@ -477,33 +473,35 @@
         )
 
     def send_back(slot, value):
-        stacked = jnp.concatenate([value[:, :half], value[:, half:]], axis=0)
-        message = dot(table["lines"][: 2 * m], stacked).astype(jnp.bfloat16)
-        back_send[slot] = message.reshape(n, 2 * ZB * rows, half)
+        for h in range(2):
+            part = value[:, h * half : (h + 1) * half].reshape(n, each, half)
+            back_send[slot, :, h * each : (h + 1) * each, :] = part.astype(jnp.bfloat16)
         scatter(back_send.at[slot], back_recv.at[slot], back_sems.at[slot], to_homes)
         own(slot).start()
 
-    send_back(0, warped)
+    send_back(0, warped_f)
     loaded("dx", "dy", "x", "fy", "by", "gain")
     slope_x = dot(table["dx"][:m], warped) + dot(table["dx"][m:], warped)
     collect(image_send.at[1], image_recv.at[1], image_sems.at[1])
-    image = dot(table["lines"][2 * m : 4 * m], image_recv[1].reshape(2 * m, half))
-    image = jnp.concatenate([image[:m], image[m:]], axis=1)
-    residual = image - warped.astype(jnp.float32)
+    image = [
+        image_recv[1, :, h * each : (h + 1) * each, :].astype(jnp.float32).reshape(m, half)
+        for h in range(2)
+    ]
+    residual = jnp.concatenate(image, axis=1) - warped_f
 
     def smooth(slot, slope):
         force = (slope * residual).astype(jnp.bfloat16)
         spectrum = dot(force, table["fy"][...]).astype(jnp.bfloat16)
         spectrum = dot(table["x"][:m], spectrum) * table["gain"][...]
         spectrum = dot(table["x"][m:], spectrum.astype(jnp.bfloat16)).astype(jnp.bfloat16)
-        send_back(slot, dot(spectrum, table["by"][...]).astype(jnp.bfloat16))
+        send_back(slot, dot(spectrum, table["by"][...]))
 
     smooth(1, slope_x)
     smooth(2, dot(warped, table["dy"][:ny]) + dot(warped, table["dy"][ny:]))
     for halo in halos:
         halo.wait_recv()
     near = jnp.concatenate([warped, halo_recv[0], halo_recv[1]], axis=0)
-    smooth(3, dot(table["lines"][4 * m :], near))
+    smooth(3, dot(table["dz"][...], near))
 
     drain(code_send, code_recv, code_sems)
     for slot in range(2):
@@ -517,48 +515,27 @@
 
 
 def finish(
-    back_hbm,
-    velocity_hbm,
-    sort_hbm,
-    warped_hbm,
-    gradient_hbm,
     back_ref,
     velocity_ref,
     sort_ref,
+    warped_hbm,
+    gradient_hbm,
     warped_ref,
     gradient_ref,
-    load_sems,
     store_sems,
 ):
     rows, planes, ny = warped_ref.shape
     m = rows * planes
-    sort = pltpu.make_async_copy(sort_hbm, sort_ref, load_sems.at[0])
-    backs = [
-        pltpu.make_async_copy(back_hbm.at[slot], back_ref.at[slot], load_sems.at[1 + slot])
-        for slot in range(4)
-    ]
-    velocities = [
-        pltpu.make_async_copy(velocity_hbm.at[c], velocity_ref.at[c], load_sems.at[5 + c])
-        for c in range(3)
-    ]
     stores = [pltpu.make_async_copy(warped_ref, warped_hbm, store_sems.at[0])] + [
         pltpu.make_async_copy(gradient_ref.at[c], gradient_hbm.at[c], store_sems.at[1 + c])
         for c in range(3)
     ]
-    sort.start()
     for slot in (1, 2, 3, 0):
-        backs[slot].start()
-        if slot > 0:
-            velocities[slot - 1].start()
-    sort.wait()
-    for slot in (1, 2, 3, 0):
-        backs[slot].wait()
         home = dot(sort_ref[...], back_ref[slot].reshape(2 * m, ny // 2))
         home = jnp.concatenate([home[:m], home[m:]], axis=1).reshape(rows, planes, ny)
         if slot == 0:
             warped_ref[...] = home.astype(jnp.bfloat16)
         else:
-            velocities[slot - 1].wait()
             gradient_ref[slot - 1] = velocity_ref[slot - 1] + home
         stores[slot].start()
     for store in stores:
@@ -610,18 +587,14 @@
             jax.ShapeDtypeStruct(template.shape, b16),
             jax.ShapeDtypeStruct(velocity.shape, f32),
         ),
-        in_specs=[hbm, hbm, hbm],
+        in_specs=[pl.BlockSpec(memory_space=pltpu.VMEM)] * 3,
         out_specs=(hbm, hbm),
         scratch_shapes=[
-            pltpu.VMEM(back.shape, b16),
-            pltpu.VMEM(velocity.shape, f32),
-            pltpu.VMEM(sort_rows.shape, b16),
             pltpu.VMEM(template.shape, b16),
             pltpu.VMEM(velocity.shape, f32),
-            pltpu.SemaphoreType.DMA((8,)),
             pltpu.SemaphoreType.DMA((4,)),
         ],
-        compiler_params=pltpu.CompilerParams(vmem_limit_bytes=60 * 1024 * 1024),
+        compiler_params=pltpu.CompilerParams(vmem_limit_bytes=12 * 1024 * 1024),
         cost_estimate=pl.CostEstimate(
             flops=16 * m * m * ny, bytes_accessed=4 * m * ny * 8, transcendentals=0
         ),

time: 31.4 us -> 30.6 us (0.975)
  Pallas kernels: 30.6 us -> 28.7 us
  local copies, waits for them, and re-layouts: 0 us -> 1.05 us
    pallas_call x1, Pallas kernels: 2.66 us -> 1.19 us  [by_groups(): pl.pallas_call(finish, out_shape=(jax.ShapeDtypeStruct(template.shape, b1...]
    unnamed x0 -> x6, local copies, waits for them, and re-layouts: none -> 1.05 us
    pallas_call x1, Pallas kernels: 27.9 us -> 27.5 us  [by_groups(): pl.pallas_call(functools.partial(body, n, names), out_shape=jax.ShapeDtyp...]
where the time goes in v6:
time: 30.6 us; the launch traced here: 30.4 us
  Pallas kernels  28.7 us (94%)
  local copies, waits for them, and re-layouts  1.05 us (3%)
  between operations  0.68 us (2%)
    pallas_call x1, Pallas kernels, by_groups(): pl.pallas_call(functools.partial(body, n, names), out_shape=jax.ShapeDtyp...  27.5 us
    pallas_call x1, Pallas kernels, by_groups(): pl.pallas_call(finish, out_shape=(jax.ShapeDtypeStruct(template.shape, b1...  1.19 us
    unnamed x6, local copies, waits for them, and re-layouts  1.05 us

profile of v6, /device:TPU:0, one launch (start us, length us, event | category | flops | bytes accessed | tf_op | source)
XLA Modules:
  0.0 30.4 jit_solution(6422955351841389207)
XLA Ops:
  0.6 0.0 copy-start.2
  0.6 0.0 copy-start.1
  0.7 27.5 %shard_map.221.back_ref = bf16[4,16,16,256]{3,2,1,0:T(8,128)(2,1)} custom-call(bf16[4,32,512]{2,1,0:T(8,128)(2,1)} %template_hbm.1, bf16[4,32,512]{2,1,0:T(8,128)(2,1)} %image_hbm.1, s32[2,256]{1,0:T(2,128)} %owner_hbm.1, s32[2,256]{1,0:T(2,128)} %offset_hbm.1, s32[2,256]{1,0:T(2,128)} %level_hbm.1, bf16[256,256]{1,0:T(8,128)(2,1)} %constant.32.clone.refs_0_, ...), custom_call_target="tpu_custom_call" | custom-call | flops 805306368 | bytes 2097152 | tf_op jit(solution)/shard_map/pallas_call | solution.py:556
  28.1 0.0 copy-done.2
  28.2 0.0 copy-done.1
  28.2 0.0 copy-start
  28.2 1.0 %copy-done = bf16[4,16,16,256]{3,2,1,0:T(8,128)(2,1)S(1)} copy-done((bf16[4,16,16,256]{3,2,1,0:T(8,128)(2,1)S(1)}, bf16[4,16,16,256]{3,2,1,0:T(8,128)(2,1)}, u32[]{:S(2)}) %copy-start) | copy-done | bytes 524312
  29.2 1.2 %shard_map.222 = (bf16[4,32,512]{2,1,0:T(8,128)(2,1)}, f32[3,4,32,512]{3,2,1,0:T(8,128)}) custom-call(bf16[4,16,16,256]{3,2,1,0:T(8,128)(2,1)S(1)} %copy-done, f32[3,4,32,512]{3,2,1,0:T(8,128)S(1)} %copy-done.1, bf16[256,256]{1,0:T(8,128)(2,1)S(1)} %copy-done.2), custom_call_target="tpu_custom_call" | custom-call | flops 134217728 | bytes 2097152 | tf_op jit(solution)/shard_map/pallas_call | solution.py:584
Async XLA Ops:
  0.6 27.5 %copy-start.2 = (bf16[256,256]{1,0:T(8,128)(2,1)S(1)}, bf16[256,256]{1,0:T(8,128)(2,1)}, u32[]{:S(2)}) copy-start(bf16[256,256]{1,0:T(8,128)(2,1)} %constant.47.clone.sort_ref) | copy-start | bytes 393220
  0.6 27.5 %copy-start.1 = (f32[3,4,32,512]{3,2,1,0:T(8,128)S(1)}, f32[3,4,32,512]{3,2,1,0:T(8,128)}, u32[]{:S(2)}) copy-start(f32[3,4,32,512]{3,2,1,0:T(8,128)} %velocity_ref.1) | copy-start | bytes 2359300
  28.2 1.0 %copy-start = (bf16[4,16,16,256]{3,2,1,0:T(8,128)(2,1)S(1)}, bf16[4,16,16,256]{3,2,1,0:T(8,128)(2,1)}, u32[]{:S(2)}) copy-start(bf16[4,16,16,256]{3,2,1,0:T(8,128)(2,1)} %shard_map.221.back_ref) | copy-start | bytes 1572868

commit v7 on v6

--- a/solution.py
+++ b/solution.py
@@ -322,8 +322,8 @@
             zip(("template", "image", "owner", "offset", "level") + names, sources, targets)
         )
     }
-    order = ("template", "early", "owner", "offset", "level", "spread", "mask", "image", "lay", "fold")
-    for key in order + tuple(key for key in names if key not in order):
+    order = ("owner", "offset", "level", "mask", "spread", "template", "early")
+    for key in order:
         loads[key].start()
 
     def loaded(*keys):
@@ -354,6 +354,9 @@
         pl.semaphore_signal(
             barrier, inc=1, device_id={"pencil": to}, device_id_type=pl.DeviceIdType.MESH
         )
+    order += ("image", "lay", "fold", "first", "second")
+    for key in order[7:] + tuple(key for key in names if key not in order):
+        loads[key].start()
 
     to_groups = [(to, flip(to), me) for to in partners]
     to_homes = [(to, to, group) for to in partners]
@@ -391,8 +394,6 @@
         message = dot(table["early"][...], stacked).astype(jnp.bfloat16)
         image_send[slot] = message.reshape(n, 2 * ZB * rows, half)
 
-    loaded("template", "early")
-    sort_image(0, template_ref)
     loaded("owner", "offset", "level", "spread", "mask")
     shift = (planes // ZB * per).bit_length() - 1
     base = owner_ref[...] * rows + lax.shift_right_logical(
@@ -406,6 +407,8 @@
     code_send[...] = codes.reshape(n, 1, 128)
     pl.semaphore_wait(barrier, n - 1)
     scatter(code_send, code_recv, code_sems, to_groups)
+    loaded("template", "early")
+    sort_image(0, template_ref)
     scatter(image_send.at[0], image_recv.at[0], image_sems.at[0], to_groups)
     code_recv[me] = code_send[group]
     image_recv[0, me] = image_send[0, group]

time: 30.6 us -> 30.9 us (level)
  Pallas kernels: 28.7 us -> 29.1 us
    pallas_call x1, Pallas kernels: 27.5 us -> 27.9 us  [by_groups(): pl.pallas_call(functools.partial(body, n, names), out_shape=jax.ShapeDtyp...]
where the time goes in v7:
time: 30.9 us; the launch traced here: 30.8 us
  Pallas kernels  29.1 us (94%)
  local copies, waits for them, and re-layouts  1.05 us (3%)
  between operations  0.68 us (2%)
    pallas_call x1, Pallas kernels, by_groups(): pl.pallas_call(functools.partial(body, n, names), out_shape=jax.ShapeDtyp...  27.9 us
    pallas_call x1, Pallas kernels, by_groups(): pl.pallas_call(finish, out_shape=(jax.ShapeDtypeStruct(template.shape, b1...  1.19 us
    unnamed x6, local copies, waits for them, and re-layouts  1.05 us

profile of v7, /device:TPU:0, one launch (start us, length us, event | category | flops | bytes accessed | tf_op | source)
XLA Modules:
  0.0 30.8 jit_solution(13855419696251512347)
XLA Ops:
  0.6 0.0 copy-start.2
  0.6 0.0 copy-start.1
  0.7 27.9 %shard_map.221.back_ref = bf16[4,16,16,256]{3,2,1,0:T(8,128)(2,1)} custom-call(bf16[4,32,512]{2,1,0:T(8,128)(2,1)} %template_hbm.1, bf16[4,32,512]{2,1,0:T(8,128)(2,1)} %image_hbm.1, s32[2,256]{1,0:T(2,128)} %owner_hbm.1, s32[2,256]{1,0:T(2,128)} %offset_hbm.1, s32[2,256]{1,0:T(2,128)} %level_hbm.1, bf16[256,256]{1,0:T(8,128)(2,1)} %constant.32.clone.refs_0_, ...), custom_call_target="tpu_custom_call" | custom-call | flops 805306368 | bytes 2097152 | tf_op jit(solution)/shard_map/pallas_call | solution.py:559
  28.5 0.0 copy-done.2
  28.5 0.0 copy-done.1
  28.5 0.0 copy-start
  28.6 1.0 %copy-done = bf16[4,16,16,256]{3,2,1,0:T(8,128)(2,1)S(1)} copy-done((bf16[4,16,16,256]{3,2,1,0:T(8,128)(2,1)S(1)}, bf16[4,16,16,256]{3,2,1,0:T(8,128)(2,1)}, u32[]{:S(2)}) %copy-start) | copy-done | bytes 524312
  29.6 1.2 %shard_map.222 = (bf16[4,32,512]{2,1,0:T(8,128)(2,1)}, f32[3,4,32,512]{3,2,1,0:T(8,128)}) custom-call(bf16[4,16,16,256]{3,2,1,0:T(8,128)(2,1)S(1)} %copy-done, f32[3,4,32,512]{3,2,1,0:T(8,128)S(1)} %copy-done.1, bf16[256,256]{1,0:T(8,128)(2,1)S(1)} %copy-done.2), custom_call_target="tpu_custom_call" | custom-call | flops 134217728 | bytes 2097152 | tf_op jit(solution)/shard_map/pallas_call | solution.py:587
Async XLA Ops:
  0.6 27.9 %copy-start.2 = (bf16[256,256]{1,0:T(8,128)(2,1)S(1)}, bf16[256,256]{1,0:T(8,128)(2,1)}, u32[]{:S(2)}) copy-start(bf16[256,256]{1,0:T(8,128)(2,1)} %constant.47.clone.sort_ref) | copy-start | bytes 393220
  0.6 27.9 %copy-start.1 = (f32[3,4,32,512]{3,2,1,0:T(8,128)S(1)}, f32[3,4,32,512]{3,2,1,0:T(8,128)}, u32[]{:S(2)}) copy-start(f32[3,4,32,512]{3,2,1,0:T(8,128)} %velocity_ref.1) | copy-start | bytes 2359300
  28.5 1.0 %copy-start = (bf16[4,16,16,256]{3,2,1,0:T(8,128)(2,1)S(1)}, bf16[4,16,16,256]{3,2,1,0:T(8,128)(2,1)}, u32[]{:S(2)}) copy-start(bf16[4,16,16,256]{3,2,1,0:T(8,128)(2,1)} %shard_map.221.back_ref) | copy-start | bytes 1572868

commit v8 on v6

--- a/solution.py
+++ b/solution.py
@@ -482,6 +482,7 @@
     send_back(0, warped_f)
     loaded("dx", "dy", "x", "fy", "by", "gain")
     slope_x = dot(table["dx"][:m], warped) + dot(table["dx"][m:], warped)
+    slope_y = dot(warped, table["dy"][:ny]) + dot(warped, table["dy"][ny:])
     collect(image_send.at[1], image_recv.at[1], image_sems.at[1])
     image = [
         image_recv[1, :, h * each : (h + 1) * each, :].astype(jnp.float32).reshape(m, half)
@@ -497,7 +498,7 @@
         send_back(slot, dot(spectrum, table["by"][...]))
 
     smooth(1, slope_x)
-    smooth(2, dot(warped, table["dy"][:ny]) + dot(warped, table["dy"][ny:]))
+    smooth(2, slope_y)
     for halo in halos:
         halo.wait_recv()
     near = jnp.concatenate([warped, halo_recv[0], halo_recv[1]], axis=0)

time: 30.6 us -> 30.6 us (level)
  no operation moved by 1% of the time
where the time goes in v8:
time: 30.6 us; the launch traced here: 30.4 us
  Pallas kernels  28.7 us (94%)
  local copies, waits for them, and re-layouts  1.05 us (3%)
  between operations  0.68 us (2%)
    pallas_call x1, Pallas kernels, by_groups(): pl.pallas_call(functools.partial(body, n, names), out_shape=jax.ShapeDtyp...  27.5 us
    pallas_call x1, Pallas kernels, by_groups(): pl.pallas_call(finish, out_shape=(jax.ShapeDtypeStruct(template.shape, b1...  1.19 us
    unnamed x6, local copies, waits for them, and re-layouts  1.05 us

profile of v8, /device:TPU:0, one launch (start us, length us, event | category | flops | bytes accessed | tf_op | source)
XLA Modules:
  0.0 30.4 jit_solution(9349407169484005744)
XLA Ops:
  0.6 0.0 copy-start.2
  0.6 0.0 copy-start.1
  0.7 27.5 %shard_map.221.back_ref = bf16[4,16,16,256]{3,2,1,0:T(8,128)(2,1)} custom-call(bf16[4,32,512]{2,1,0:T(8,128)(2,1)} %template_hbm.1, bf16[4,32,512]{2,1,0:T(8,128)(2,1)} %image_hbm.1, s32[2,256]{1,0:T(2,128)} %owner_hbm.1, s32[2,256]{1,0:T(2,128)} %offset_hbm.1, s32[2,256]{1,0:T(2,128)} %level_hbm.1, bf16[256,256]{1,0:T(8,128)(2,1)} %constant.32.clone.refs_0_, ...), custom_call_target="tpu_custom_call" | custom-call | flops 805306368 | bytes 2097152 | tf_op jit(solution)/shard_map/pallas_call | solution.py:557
  28.1 0.0 copy-done.2
  28.2 0.0 copy-done.1
  28.2 0.0 copy-start
  28.2 1.0 %copy-done = bf16[4,16,16,256]{3,2,1,0:T(8,128)(2,1)S(1)} copy-done((bf16[4,16,16,256]{3,2,1,0:T(8,128)(2,1)S(1)}, bf16[4,16,16,256]{3,2,1,0:T(8,128)(2,1)}, u32[]{:S(2)}) %copy-start) | copy-done | bytes 524312
  29.2 1.2 %shard_map.222 = (bf16[4,32,512]{2,1,0:T(8,128)(2,1)}, f32[3,4,32,512]{3,2,1,0:T(8,128)}) custom-call(bf16[4,16,16,256]{3,2,1,0:T(8,128)(2,1)S(1)} %copy-done, f32[3,4,32,512]{3,2,1,0:T(8,128)S(1)} %copy-done.1, bf16[256,256]{1,0:T(8,128)(2,1)S(1)} %copy-done.2), custom_call_target="tpu_custom_call" | custom-call | flops 134217728 | bytes 2097152 | tf_op jit(solution)/shard_map/pallas_call | solution.py:585
Async XLA Ops:
  0.6 27.5 %copy-start.2 = (bf16[256,256]{1,0:T(8,128)(2,1)S(1)}, bf16[256,256]{1,0:T(8,128)(2,1)}, u32[]{:S(2)}) copy-start(bf16[256,256]{1,0:T(8,128)(2,1)} %constant.47.clone.sort_ref) | copy-start | bytes 393220
  0.6 27.5 %copy-start.1 = (f32[3,4,32,512]{3,2,1,0:T(8,128)S(1)}, f32[3,4,32,512]{3,2,1,0:T(8,128)}, u32[]{:S(2)}) copy-start(f32[3,4,32,512]{3,2,1,0:T(8,128)} %velocity_ref.1) | copy-start | bytes 2359300
  28.2 1.0 %copy-start = (bf16[4,16,16,256]{3,2,1,0:T(8,128)(2,1)S(1)}, bf16[4,16,16,256]{3,2,1,0:T(8,128)(2,1)}, u32[]{:S(2)}) copy-start(bf16[4,16,16,256]{3,2,1,0:T(8,128)(2,1)} %shard_map.221.back_ref) | copy-start | bytes 1572868
